TPU v7x, 32 devices: a whole 2x2x4 slice. The times are simulated.
32 devices in a mesh: dp: 16 (over z, y, core), mp: 2 (over x).
Axes of the slice: x: 2, y: 2, z: 4, core: 2. Of those that a mesh axis runs over, the one named last changes fastest.
Arguments:
- state: bfloat16 [32768, 512], P('dp'), may hold values from -6 to 6
- lengths: int32 [32], P('dp'), may hold values from 256 to 1024, as said below
- halt_mask: int32 [32768], P('dp'), may hold values 0 or 1
- w_query: bfloat16 [512, 512], P(None, 'mp'), may hold values from -0.25 to 0.25
- w_key: bfloat16 [512, 512], P(None, 'mp'), may hold values from -0.25 to 0.25
- w_value: bfloat16 [512, 512], P(None, 'mp'), may hold values from -0.25 to 0.25
- w_output: bfloat16 [512, 512], P('mp'), may hold values from -1 to 1
- first_norm_gain: float32 [512], replicated, may hold values from 0.1 to 1.9
- first_norm_bias: float32 [512], replicated, may hold values from -3 to 3
- w_inner: bfloat16 [512, 2048], P(None, 'mp'), may hold values from -0.25 to 0.25
- w_outer: bfloat16 [2048, 512], P('mp'), may hold values from -0.125 to 0.125
- second_norm_gain: float32 [512], replicated, may hold values from 0.1 to 1.9
- second_norm_bias: float32 [512], replicated, may hold values from -3 to 3
- halt_weight: float32 [512], replicated, may hold values from -0.25 to 0.25
- cotangent: bfloat16 [32768, 512], P('dp'), may hold values from -6 to 6
Outputs:
- new_state: float32 [32768, 512], P('dp')
- grad_state: float32 [32768, 512], P('dp')
- grad_query: float32 [512, 512], P(None, 'mp')
- grad_key: float32 [512, 512], P(None, 'mp')
- grad_value: float32 [512, 512], P(None, 'mp')
- grad_output: float32 [512, 512], P('mp')
- first_gain_gradient: float32 [512], replicated
- grad_bias1: float32 [512], replicated
- grad_inner: float32 [512, 2048], P(None, 'mp')
- grad_outer: float32 [2048, 512], P('mp')
- second_gain_gradient: float32 [512], replicated
- grad_bias2: float32 [512], replicated
- grad_halt: float32 [512], replicated
Inputs may be any that keep to these rules, and one draw needn't show every extreme that they name: Tokens of sequence s at positions lengths[s] and beyond are padding; some sequence has exactly 1024 real tokens.
All inputs are finite; a program needn't handle non-finite values. No bound on the sum of `halt_mask` on one device may be relied on, other than what follows from the above.
Results may differ from a plain program's by a relative error of at most 0.017.
The roundings to bfloat16 on the way count: a program that leaves them out, or rounds other values in their place, can miss the bound.
Values sent between devices are 32-bit elements; how exact they have to be, the bound alone decides.
No kernel may reach another device: no remote copies, remote signals or barrier semaphores. Data moves between devices by JAX's collectives and lax.ppermute only.
A program may use at most 256 MiB of HBM per device.

v0:
```python
import functools
import math

import jax
import jax.numpy as jnp
import numpy as np
from jax import lax
from jax.experimental import pallas as pl
from jax.experimental.pallas import tpu as pltpu
from jax.sharding import PartitionSpec as P

HEAD = 64
LEN = 1024
STEP = 2
LOG2E = 1.4426950408889634
BF = jnp.bfloat16
F32 = jnp.float32
NN = (((1,), (0,)), ((), ()))
NT = (((1,), (1,)), ((), ()))
TN = (((0,), (0,)), ((), ()))
TT = (((0,), (1,)), ((), ()))
VMEM_LIMIT = 60 << 20
CHUNK = 256
SUBS = 2


def mm(a, b, dims=NN):
    return lax.dot_general(a, b, dims, preferred_element_type=F32)


def params():
    return pltpu.CompilerParams(vmem_limit_bytes=VMEM_LIMIT)


def whole(shape):
    zeros = (0,) * len(shape)
    return pl.BlockSpec(shape, lambda *_: zeros)


def timing_rows(width):
    half = width // 2
    rates = np.exp(-math.log(10000.0) * np.arange(half, dtype=np.float64) / (half - 1))

    def rows(positions):
        angles = positions[:, None] * rates[None, :]
        return np.concatenate([np.sin(angles), np.cos(angles)], axis=1)

    return (rows(np.arange(LEN, dtype=np.float64)) + rows(np.array([float(STEP)]))).astype(
        np.float32
    )


def split_low(value):
    high = value.astype(BF)
    return high, (value - high.astype(F32)).astype(BF)


def rolled(pair):
    return jnp.concatenate([pair[:, HEAD:], pair[:, :HEAD]], axis=1)


def lane_index(shape):
    return lax.broadcasted_iota(jnp.int32, shape, 1)


def row_index(shape):
    return lax.broadcasted_iota(jnp.int32, shape, 0)


def attention_forward_kernel(seq, lengths, x_in, wq, wk, wv, *rest, heads):
    e_out, mixed_out, r_out, kaug, qaug, vaug, sa, sb, ma, mb = rest[-10:]
    j = pl.program_id(0)
    last = heads // 2 - 1
    pieces = LEN // CHUNK

    def score_piece(i, c, target):
        rows = slice(c * CHUNK, (c + 1) * CHUNK)
        s = mm(kaug[i, rows], qaug[i])
        target[rows] = s
        return jnp.max(s.reshape(CHUNK // 8, 8, LEN), axis=0)

    @pl.when(j == 0)
    def _():
        x = x_in[...]
        query = mm(wq[...], x, TT).astype(BF).astype(F32) * (LOG2E / math.sqrt(HEAD))
        high, rest = split_low(query)
        key = mm(x, wk[...]).astype(BF)
        value = mm(wv[...], x, TT).astype(BF)
        shape = (LEN, 2 * HEAD)
        lane = lane_index(shape)
        padded = row_index(shape) >= lengths[seq]
        mask = jnp.where(padded & ((lane == 0) | (lane == HEAD)), -1e30, 0.0).astype(BF)
        first = row_index((HEAD, LEN)) == 0
        ones = jnp.where(first, 1.0, 0.0).astype(BF)
        zeros = jnp.zeros((HEAD, LEN), BF)
        for i in range(heads):
            pair = key[:, (i // 2) * 128 : (i // 2) * 128 + 128]
            turned = rolled(pair)
            mine = slice(i * HEAD, (i + 1) * HEAD)
            kaug[i, :, 0:128] = pair
            if i % 2 == 0:
                kaug[i, :, 128:256] = jnp.where(lane < HEAD, mask, turned)
                parts = (high[mine], zeros, ones, rest[mine])
            else:
                kaug[i, :, 128:256] = jnp.where(lane < HEAD, turned, mask)
                parts = (zeros, high[mine], rest[mine], ones)
            for n, part in enumerate(parts):
                qaug[i, n * HEAD : (n + 1) * HEAD] = part
            vaug[i, 0:HEAD] = value[mine]
            vaug[i, HEAD : HEAD + 16] = jnp.ones((16, LEN), BF)
        top = None
        for c in range(pieces):
            m = score_piece(0, c, sa)
            top = m if top is None else jnp.maximum(top, m)
        ma[...] = jnp.max(top, axis=0, keepdims=True)

    def step(slot, cur, cur_m, nxt, nxt_m, ahead=True):
        i = 2 * j + slot
        shift = cur_m[...]
        top = None
        out = None
        for c in range(pieces):
            rows = slice(c * CHUNK, (c + 1) * CHUNK)
            if ahead:
                m = score_piece(i + 1, c, nxt)
                top = m if top is None else jnp.maximum(top, m)
            e = jnp.exp2(cur[rows] - shift).astype(BF)
            e_out[slot, rows] = e
            o = mm(vaug[i, :, rows], e)
            out = o if out is None else out + o
        if ahead:
            nxt_m[...] = jnp.max(top, axis=0, keepdims=True)
        r = 1.0 / out[HEAD : HEAD + 1]
        mixed_out[slot * HEAD : (slot + 1) * HEAD] = (out[:HEAD] * r).astype(BF)
        r_out[slot] = r

    step(0, sa, ma, sb, mb)

    @pl.when(j < last)
    def _():
        step(1, sb, mb, sa, ma)

    @pl.when(j == last)
    def _():
        step(1, sb, mb, sa, ma, ahead=False)


def attention_forward(seq, lengths, x, wq, wk, wv, earlier=()):
    rows, width = x.shape
    local = wq.shape[1]
    heads = local // HEAD
    steps, total = heads // 2, rows // LEN * heads
    return pl.pallas_call(
        functools.partial(attention_forward_kernel, seq, heads=heads),
        grid=(steps,),
        in_specs=[
            pl.BlockSpec(memory_space=pltpu.SMEM),
            pl.BlockSpec((LEN, width), lambda j: (seq, 0)),
            whole((width, local)),
            whole((width, local)),
            whole((width, local)),
        ]
        + [pl.BlockSpec(memory_space=pl.ANY)] * len(earlier),
        out_specs=[
            pl.BlockSpec((2, LEN, LEN), lambda j: (seq * steps + j, 0, 0)),
            pl.BlockSpec((2 * HEAD, LEN), lambda j: (j, seq)),
            pl.BlockSpec((2, 1, LEN), lambda j: (seq * steps + j, 0, 0)),
        ],
        out_shape=[
            jax.ShapeDtypeStruct((total, LEN, LEN), BF),
            jax.ShapeDtypeStruct((local, rows), BF),
            jax.ShapeDtypeStruct((total, 1, LEN), F32),
        ],
        scratch_shapes=[
            pltpu.VMEM((heads, LEN, 256), BF),
            pltpu.VMEM((heads, 256, LEN), BF),
            pltpu.VMEM((heads, HEAD + 16, LEN), BF),
            pltpu.VMEM((LEN, LEN), F32),
            pltpu.VMEM((LEN, LEN), F32),
            pltpu.VMEM((1, LEN), F32),
            pltpu.VMEM((1, LEN), F32),
        ],
        compiler_params=params(),
        input_output_aliases={5 + n: n for n in range(len(earlier))},
        cost_estimate=pl.CostEstimate(
            flops=8 * 2 * heads * LEN * LEN * HEAD,
            bytes_accessed=2 * heads * LEN * LEN,
            transcendentals=heads * LEN * LEN,
        ),
        name="attention_forward",
    )(lengths, x, wq, wk, wv, *earlier)


def row_mean(v):
    return jnp.mean(v, axis=-1, keepdims=True)


def norm_rows(v):
    centre = v - row_mean(v)
    deviation = lax.rsqrt(row_mean(centre * centre) + 1e-05)
    return centre * deviation, deviation


def norm_back(e, xhat, deviation):
    return deviation * (e - row_mean(e) - xhat * row_mean(e * xhat))


def fold_rows(v):
    return jnp.sum(v.reshape(v.shape[0] // 8, 8, v.shape[1]), axis=0)


def middle_kernel(
    state, timing, cot, run, mix_a, mix_b, r_a, r_b, wo_a, wo_b, wi_a, wi_b, wu_a, wu_b,
    vectors, new_state, gs, do_a, do_b, dl_a, dl_b, gu, gi, go, act, slope, inner_low, low1,
    out_low, att_low, fold, *, heads
):
    t = pl.program_id(0)
    last = pl.num_programs(0) - 1
    tile = state.shape[0]
    size = tile // SUBS
    local = wo_a.shape[0]
    gain1, bias1, gain2, bias2, halt_w = (vectors[n : n + 1] for n in range(5))
    c0 = math.sqrt(2.0 / math.pi)
    halves = ((wi_a, wu_a), (wi_b, wu_b))
    running_column = jnp.broadcast_to(run[0].astype(F32), (8, tile)).T[:, 0:1]

    @pl.when(t == 0)
    def _():
        for ref in (gu, gi, go, fold):
            ref[...] = jnp.zeros(ref.shape, F32)

    def first_norm(k):
        rows = slice(k * size, (k + 1) * size)
        embedded = state[rows].astype(F32) + timing[rows]
        attended = mm(mix_a[:, rows], wo_a[...], TN) + mm(mix_b[:, rows], wo_b[...], TN)
        xhat1, dev1 = norm_rows(embedded + attended)
        normed1 = xhat1 * gain1 + bias1
        low1[rows] = normed1.astype(BF)
        return xhat1, dev1, normed1

    def forward(k, normed1):
        rows = slice(k * size, (k + 1) * size)
        total = normed1
        for n, (wi, wu) in enumerate(halves):
            v = mm(low1[rows], wi[...])
            square = v * v
            h = 0.5 + 0.5 * jnp.tanh(v * (c0 + (c0 * 0.044715) * square))
            g = v * h
            act[n, rows] = g.astype(BF)
            slope[n, rows] = h + g * (1.0 - h) * (2.0 * c0 + (6.0 * c0 * 0.044715) * square)
            total = total + mm(act[n, rows], wu[...])
        return total

    def second_norm(k, hidden2):
        rows = slice(k * size, (k + 1) * size)
        old = state[rows].astype(F32)
        xhat2, dev2 = norm_rows(hidden2)
        block = xhat2 * gain2 + bias2
        halt = jax.nn.sigmoid(jnp.sum(block * halt_w, axis=-1, keepdims=True))
        running = running_column[rows]
        gate = running * halt
        change = block - old
        new_state[rows] = old + gate * change
        g_in = cot[rows].astype(F32)
        d_prob = running * jnp.sum(g_in * change, axis=-1, keepdims=True)
        d_logit = d_prob * halt * (1.0 - halt)
        d_block = gate * g_in + d_logit * halt_w
        fold[4] += fold_rows(d_logit * block)
        fold[2] += fold_rows(d_block * xhat2)
        fold[3] += fold_rows(d_block)
        gs[rows] = g_in * (1.0 - gate)
        d_hidden2 = norm_back(d_block * gain2, xhat2, dev2)
        out_low[rows] = d_hidden2.astype(BF)
        return d_hidden2

    def backward(k, d_hidden2):
        rows = slice(k * size, (k + 1) * size)
        total = d_hidden2
        for n, (wi, wu) in enumerate(halves):
            d_act = mm(out_low[rows], wu[...], NT)
            inner_low[n, rows] = (d_act * slope[n, rows]).astype(BF)
            total = total + mm(inner_low[n, rows], wi[...], NT)
        return total

    def first_back(k, d_normed1, xhat1, dev1):
        rows = slice(k * size, (k + 1) * size)
        fold[0] += fold_rows(d_normed1 * xhat1)
        fold[1] += fold_rows(d_normed1)
        d_hidden1 = norm_back(d_normed1 * gain1, xhat1, dev1)
        att_low[rows] = d_hidden1.astype(BF)
        gs[rows] += d_hidden1

    def mixed_back():
        for mix, r, wo, do, dl in (
            (mix_a, r_a, wo_a, do_a, dl_a),
            (mix_b, r_b, wo_b, do_b, dl_b),
        ):
            d_mixed = mm(wo[...], att_low[...], NT).astype(BF).astype(F32)
            for h in range(heads):
                mine = slice(h * HEAD, (h + 1) * HEAD)
                part = d_mixed[mine]
                scale = r[h]
                do[mine] = part * scale
                total = jnp.sum(part * mix[mine].astype(F32), axis=0, keepdims=True)
                dl[h] = total * scale

    ks = range(SUBS)
    firsts = [first_norm(k) for k in ks]
    hidden2 = {0: forward(0, firsts[0][2])}
    d_hidden2, d_normed1 = {}, {}
    for k in ks:
        d_hidden2[k] = second_norm(k, hidden2[k])
        if k + 1 < SUBS:
            hidden2[k + 1] = forward(k + 1, firsts[k + 1][2])
    d_normed1[0] = backward(0, d_hidden2[0])
    for k in ks:
        first_back(k, d_normed1[k], *firsts[k][:2])
        if k + 1 < SUBS:
            d_normed1[k + 1] = backward(k + 1, d_hidden2[k + 1])
    gu[...] += mm(act[0], out_low[...], TN)
    gi[...] += mm(low1[...], inner_low[0], TN)
    go[:local] += mm(mix_a[...], att_low[...])
    mixed_back()

    @pl.when(t == last)
    def _():
        for n in range(8):
            go[local + n : local + n + 1] = jnp.sum(fold[n], axis=0, keepdims=True)


def middle(state, timing, cot, run, mix_a, mix_b, r_a, r_b, wo_a, wo_b, wi_a, wi_b, wu_a,
           wu_b, vectors):
    rows, width = state.shape
    local, ff = wo_a.shape[0], wi_a.shape[1]
    heads = local // HEAD
    tile = 512
    per = LEN // tile
    by_rows = pl.BlockSpec((tile, width), lambda t: (t, 0))
    by_columns = pl.BlockSpec((local, tile), lambda t: (0, t))
    per_head = pl.BlockSpec((heads, 1, tile), lambda t: (t // per, 0, t % per))
    return pl.pallas_call(
        functools.partial(middle_kernel, heads=heads),
        grid=(rows // tile,),
        in_specs=[
            by_rows,
            pl.BlockSpec((tile, width), lambda t: (t % per, 0)),
            by_rows,
            pl.BlockSpec((1, 1, tile), lambda t: (t, 0, 0)),
            by_columns,
            by_columns,
            per_head,
            per_head,
            whole((local, width)),
            whole((local, width)),
            whole((width, ff)),
            whole((width, ff)),
            whole((ff, width)),
            whole((ff, width)),
            whole((8, width)),
        ],
        out_specs=[
            by_rows,
            by_rows,
            by_columns,
            by_columns,
            per_head,
            per_head,
            whole((ff, width)),
            whole((width, ff)),
            whole((local + 8, width)),
        ],
        out_shape=[
            jax.ShapeDtypeStruct((rows, width), F32),
            jax.ShapeDtypeStruct((rows, width), F32),
            jax.ShapeDtypeStruct((local, rows), F32),
            jax.ShapeDtypeStruct((local, rows), F32),
            jax.ShapeDtypeStruct((rows // LEN * heads, 1, LEN), F32),
            jax.ShapeDtypeStruct((rows // LEN * heads, 1, LEN), F32),
            jax.ShapeDtypeStruct((ff, width), F32),
            jax.ShapeDtypeStruct((width, ff), F32),
            jax.ShapeDtypeStruct((local + 8, width), F32),
        ],
        scratch_shapes=[
            pltpu.VMEM((2, tile, ff), BF),
            pltpu.VMEM((2, tile, ff), F32),
            pltpu.VMEM((2, tile, ff), BF),
            pltpu.VMEM((tile, width), BF),
            pltpu.VMEM((tile, width), BF),
            pltpu.VMEM((tile, width), BF),
            pltpu.VMEM((8, 8, width), F32),
        ],
        compiler_params=params(),
        cost_estimate=pl.CostEstimate(
            flops=2 * rows * width * ff * 10 + 2 * rows * width * local * 6,
            bytes_accessed=rows * width * 20,
            transcendentals=2 * rows * ff,
        ),
        name="middle",
    )(state, timing, cot, run.reshape(rows // tile, 1, tile), mix_a, mix_b, r_a, r_b, wo_a, wo_b, wi_a, wi_b, wu_a, wu_b,
      vectors)


def attention_backward_kernel(
    core, e_in, do_in, dl_in, x_in, wq, wk, wv, gs_in, gs_out, *rest, heads, own
):
    if own:
        keep, send, gqkv, qt, kt, vaug, dq, dk, dv = rest
    else:
        qt, kt, vaug, dq, dk, dv = rest
    s, h = pl.program_id(0), pl.program_id(1)
    factor = 1.0 / math.sqrt(HEAD)
    pieces = LEN // CHUNK
    local = wq.shape[1]

    @pl.when(h == 0)
    def _():
        x = x_in[...]
        query = mm(wq[...], x, TT).astype(BF)
        key = mm(wk[...], x, TT).astype(BF)
        value = mm(x, wv[...]).astype(BF)
        lane = lane_index((LEN, 2 * HEAD))
        ones = jnp.where((lane % HEAD) < 3, 1.0, 0.0).astype(BF)
        for n in range(heads):
            mine = slice(n * HEAD, (n + 1) * HEAD)
            qt[n] = query[mine]
            kt[n] = key[mine]
            pair = value[:, (n // 2) * 128 : (n // 2) * 128 + 128]
            turned = rolled(pair)
            if n % 2 == 0:
                vaug[n, :, 0:128] = jnp.where(lane < HEAD, pair, turned)
            else:
                vaug[n, :, 0:128] = jnp.where(lane < HEAD, turned, pair)
            vaug[n, :, 128:256] = ones

    high, low = split_low(do_in[...])
    delta = -dl_in[0]
    d1 = delta.astype(BF)
    left = delta - d1.astype(F32)
    d2 = left.astype(BF)
    d3 = (left - d2.astype(F32)).astype(BF)
    index = row_index((2 * HEAD, LEN))
    tail = jnp.where(
        index == 0,
        d1.astype(F32),
        jnp.where(index == 1, d2.astype(F32), jnp.where(index == 2, d3.astype(F32), 0.0)),
    ).astype(BF)
    right = jnp.concatenate([high, low, tail], axis=0)
    query = qt[h]
    out = None
    for c in range(pieces):
        rows = slice(c * CHUNK, (c + 1) * CHUNK)
        d_probs = mm(vaug[h, rows], right)
        e = e_in[0, rows]
        d_scores = (e.astype(F32) * d_probs).astype(BF)
        dv[h, rows] = mm(e, high, NT).astype(BF)
        dk[h, rows] = (mm(d_scores, query, NT) * factor).astype(BF)
        o = mm(kt[h, :, rows], d_scores)
        out = o if out is None else out + o
    dq[pl.ds(pl.multiple_of(h * HEAD, HEAD), HEAD)] = (out * factor).astype(BF)

    @pl.when(h == heads - 1)
    def _():
        d_query = dq[...]
        d_key = jnp.concatenate([dk[n] for n in range(heads)], axis=1)
        d_value = jnp.concatenate([dv[n] for n in range(heads)], axis=1)
        total = mm(d_query, wq[...], TT)
        total = total + mm(d_key, wk[...], NT)
        total = total + mm(d_value, wv[...], NT)
        gs_out[...] = gs_in[...] + total
        if own:
            x = x_in[...]
            g1 = mm(d_query, x).T
            g2 = mm(x, jnp.concatenate([d_key, d_value], axis=1), TN)

            @pl.when(s == 0)
            def _():
                gqkv[:, :local] = g1
                gqkv[:, local:] = g2

            @pl.when(s > 0)
            def _():
                gqkv[:, :local] += g1
                gqkv[:, local:] += g2

            @pl.when(s == pl.num_programs(0) - 1)
            def _():
                half = keep.shape[0]
                keep[...] = gqkv[rows_at(core[0], half)]
                send[...] = gqkv[rows_at(1 - core[0], half)]


def attention_backward(first, seqs, core, e, do, dl, x, wq, wk, wv, gs, own):
    rows, width = x.shape
    local = wq.shape[1]
    heads = local // HEAD
    by_rows = pl.BlockSpec((LEN, width), lambda s, h: (first + s, 0))
    out_specs = [by_rows]
    out_shape = [jax.ShapeDtypeStruct((rows, width), F32)]
    scratch = []
    if own:
        out_specs += [whole((width // 2, 3 * local))] * 2
        out_shape += [jax.ShapeDtypeStruct((width // 2, 3 * local), F32)] * 2
        scratch = [pltpu.VMEM((width, 3 * local), F32)]
    return pl.pallas_call(
        functools.partial(attention_backward_kernel, heads=heads, own=own),
        grid=(seqs, heads),
        in_specs=[
            pl.BlockSpec(memory_space=pltpu.SMEM),
            pl.BlockSpec((1, LEN, LEN), lambda s, h: ((first + s) * heads + h, 0, 0)),
            pl.BlockSpec((HEAD, LEN), lambda s, h: (h, first + s)),
            pl.BlockSpec((1, 1, LEN), lambda s, h: ((first + s) * heads + h, 0, 0)),
            by_rows,
            whole((width, local)),
            whole((width, local)),
            whole((width, local)),
            by_rows,
        ],
        out_specs=out_specs,
        out_shape=out_shape,
        scratch_shapes=scratch
        + [
            pltpu.VMEM((heads, HEAD, LEN), BF),
            pltpu.VMEM((heads, HEAD, LEN), BF),
            pltpu.VMEM((heads, LEN, 256), BF),
            pltpu.VMEM((local, LEN), BF),
            pltpu.VMEM((heads, LEN, HEAD), BF),
            pltpu.VMEM((heads, LEN, HEAD), BF),
        ],
        compiler_params=params(),
        input_output_aliases={8: 0},
        cost_estimate=pl.CostEstimate(
            flops=32 * 2 * seqs * heads * LEN * LEN * HEAD, bytes_accessed=1000,
            transcendentals=0,
        ),
        name="attention_backward_own" if own else "attention_backward_other",
    )(core, e, do, dl, x, wq, wk, wv, gs)


def rows_at(index, size):
    return pl.ds(pl.multiple_of(index * size, size), size)


def local_kernel(fn, count, place, *refs):
    fn(place, refs[:count], refs[count:])


def local_call(name, fn, place, ins, outs):
    return pl.pallas_call(
        functools.partial(local_kernel, fn, len(ins)),
        in_specs=[pl.BlockSpec(memory_space=pltpu.SMEM)]
        + [pl.BlockSpec(memory_space=pltpu.VMEM)] * len(ins),
        out_specs=[pl.BlockSpec(memory_space=pltpu.VMEM)] * len(outs),
        out_shape=[jax.ShapeDtypeStruct(shape, kind) for shape, kind in outs],
        compiler_params=params(),
        name=name,
    )(place, *ins)


def cut_call(name, fn, place, ins, outs):
    return pl.pallas_call(
        functools.partial(local_kernel, fn, len(ins)),
        grid_spec=pltpu.PrefetchScalarGridSpec(
            num_scalar_prefetch=1,
            grid=(1,),
            in_specs=[
                pl.BlockSpec((v.shape[0] // 4, v.shape[1]), lambda _, p: (p[0], 0)) for v in ins
            ],
            out_specs=[pl.BlockSpec(shape, lambda _, p: (0, 0)) for shape in outs],
        ),
        out_shape=[jax.ShapeDtypeStruct(shape, F32) for shape in outs],
        compiler_params=params(),
        name=name,
    )(place, *ins)


def pack_qkv(place, ins, outs):
    local = ins[0].shape[1]
    for n, ref in enumerate(ins):
        outs[0][:, n * local : (n + 1) * local] = ref[...].astype(F32)


def pack_ff(place, ins, outs):
    wo, wi, wu = ins
    quarter, width = wi.shape[0], wo.shape[1]
    blocks = wi.shape[1] // width
    for n in range(blocks):
        outs[0][n * quarter : (n + 1) * quarter] = wi[:, n * width : (n + 1) * width].astype(F32)
    outs[0][blocks * quarter :] = wo[...].astype(F32)
    outs[1][...] = wu[...].astype(F32)


def embed_kernel(state, timing, out):
    out[...] = (state[...].astype(F32) + timing[...]).astype(BF)


def embed(state, timing):
    rows, width = state.shape
    tile = 512
    per = LEN // tile
    by_rows = pl.BlockSpec((tile, width), lambda p, s: (s * per + p, 0))
    return pl.pallas_call(
        embed_kernel,
        grid=(per, rows // LEN),
        in_specs=[by_rows, pl.BlockSpec((tile, width), lambda p, s: (p, 0))],
        out_specs=by_rows,
        out_shape=jax.ShapeDtypeStruct((rows, width), BF),
        compiler_params=params(),
        name="embed",
    )(state, timing)


def unpack_qkv(place, ins, outs):
    local = outs[0].shape[1]
    for p, ref in zip((0, 2, 1, 3), ins):
        rows = rows_at(place[p], ref.shape[0])
        for n, out in enumerate(outs):
            out[rows] = ref[:, n * local : (n + 1) * local].astype(BF)


def unpack_inner(place, ins, outs):
    wo, wi = outs
    width = wi.shape[0]
    quarter, blocks = width // 4, wi.shape[1] // width
    for p, ref in zip((0, 2, 1, 3), ins):
        rows = rows_at(place[p], quarter)
        for n in range(blocks):
            wi[rows, n * width : (n + 1) * width] = ref[
                n * quarter : (n + 1) * quarter
            ].astype(BF)
        wo[rows_at(place[p], wo.shape[0] // 4)] = ref[blocks * quarter :].astype(BF)


def unpack_outer(place, ins, outs):
    for p, ref in zip((0, 2, 1, 3), ins):
        outs[0][rows_at(place[p], ref.shape[0])] = ref[...].astype(BF)


def finish_qkv(place, ins, outs):
    local = outs[0].shape[1]
    for flip, ref in enumerate(ins):
        rows = rows_at(jnp.bitwise_xor(place[4], flip), ref.shape[0])
        for n, out in enumerate(outs):
            out[rows] = ref[:, n * local : (n + 1) * local]


def finish_ff_kernel(gu_in, gi_in, go_in, gu, gi, go, *vec):
    gu[...] = gu_in[...]
    gi[...] = gi_in[...]

    @pl.when(pl.program_id(0) == 0)
    def _():
        local = go.shape[0]
        go[...] = go_in[:local]
        for n, out in enumerate(vec):
            out[...] = go_in[local + n]


def finish_ff(gu, gi, go):
    ff, width = gu.shape
    local = go.shape[0] - 8
    steps = 4
    upper = pl.BlockSpec((ff // steps, width), lambda i: (i, 0))
    inner = pl.BlockSpec((width // steps, ff), lambda i: (i, 0))
    return pl.pallas_call(
        finish_ff_kernel,
        grid=(steps,),
        in_specs=[upper, inner, whole(go.shape)],
        out_specs=[upper, inner, whole((local, width))] + [whole((width,))] * 5,
        out_shape=[
            jax.ShapeDtypeStruct(shape, F32)
            for shape in [gu.shape, gi.shape, (local, width)] + [(width,)] * 5
        ],
        compiler_params=params(),
        name="finish_ff",
    )(gu, gi, go)


def flipped(size, even, odd):
    return [(i, i ^ (odd if i & 1 else even)) for i in range(size)]


def shards(
    dp, state, lengths, halt_mask, wq, wk, wv, wo, gain1, bias1, wi, wu, gain2, bias2,
    halt_weight, cotangent
):
    rows, width = state.shape
    local, ff = wq.shape[1], wi.shape[1]
    timing = jnp.asarray(timing_rows(width))
    me = lax.axis_index("dp").astype(jnp.int32)
    mask = np.array([3, 3, 3, 3, 1], np.int32)
    flip = np.array([0, 1, 2, 3, 0], np.int32)
    place = jnp.bitwise_xor(jnp.bitwise_and(me, mask), flip)
    bits = dp.bit_length() - 1
    tie = lax.optimization_barrier
    call = functools.partial(local_call, place=place)

    def across(v):
        return lax.ppermute(v, "mp", [(0, 1), (1, 0)])

    def along(v, even, odd=None):
        return lax.ppermute(v, "dp", flipped(dp, even, odd or even))

    quarter = width // 4
    (chunk_a,) = cut_call("pack_qkv", pack_qkv, place, (wq, wk, wv), [(quarter, 3 * local)])
    qkv0 = across(chunk_a)
    chunk_b, chunk_c = cut_call(
        "pack_ff", pack_ff, place, (wo, wi, wu),
        [(ff // 4 + local // 4, width), (ff // 4, width)],
    )
    x = embed(state, timing)
    chunk_b, x = tie((chunk_b, x))
    in0 = across(chunk_b)
    vectors = jnp.stack([gain1, bias1, gain2, bias2, halt_weight] + [gain1] * 3)
    fwd = attention_forward(0, lengths, x, wq, wk, wv)
    qkv0, chunk_c, vectors, fwd = tie((qkv0, chunk_c, vectors, fwd))
    qkv1 = along(qkv0, 2)
    out0 = across(chunk_c)
    fwd = attention_forward(1, lengths, x, wq, wk, wv, fwd)
    qkv1, in0, fwd = tie((qkv1, in0, fwd))
    qkv2, qkv3 = along(qkv0, 1), along(qkv1, 1)
    in1 = along(in0, 2)
    wq2, wk2, wv2 = call(
        "unpack_qkv", unpack_qkv, ins=(qkv0, qkv1, qkv2, qkv3),
        outs=[((width, local), BF)] * 3,
    )
    fwd2 = attention_forward(0, lengths, x, wq2, wk2, wv2)
    in1, out0, fwd2 = tie((in1, out0, fwd2))
    in2, in3 = along(in0, 1), along(in1, 1)
    out1 = along(out0, 2)
    out2 = along(out0, 1)
    fwd2 = attention_forward(1, lengths, x, wq2, wk2, wv2, fwd2)
    in2, in3, out2, fwd2 = tie((in2, in3, out2, fwd2))
    wo2, wi2 = call(
        "unpack_inner", unpack_inner, ins=(in0, in1, in2, in3),
        outs=[((local, width), BF), ((width, ff), BF)],
    )
    out1, wo2, wi2 = tie((out1, wo2, wi2))
    out3 = along(out1, 1)
    (wu2,) = call(
        "unpack_outer", unpack_outer, ins=(out0, out1, out2, out3), outs=[((ff, width), BF)]
    )
    e_a, mix_a, r_a = fwd
    e_b, mix_b, r_b = fwd2
    new_state, gs, do_a, do_b, dl_a, dl_b, *grads = middle(
        state, timing, cotangent, halt_mask, mix_a, mix_b, r_a, r_b, wo, wo2, wi, wi2, wu, wu2,
        vectors
    )

    grads = lax.psum(tuple(grads), "dp")
    own = dict(core=place[4:], e=e_a, do=do_a, dl=dl_a, x=x, wq=wq, wk=wk, wv=wv)
    other = dict(core=place[4:], e=e_b, do=do_b, dl=dl_b, x=x, wq=wq2, wk=wk2, wv=wv2)

    def attention_and_sums(carry):
        step, gs, *_ = carry
        back = attention_backward
        gs, keep, send = back(0, rows // LEN, gs=gs, own=True, **own)
        g = keep + along(send, 1)
        g, gs = tie((g, gs))
        got = along(g, 2, 4)
        (gs,) = back(0, 1, gs=gs, own=False, **other)
        got, gs = tie((got, gs))
        g = g + got
        g, gs = tie((g, gs))
        got = along(g, 4, 8)
        (gs,) = back(1, rows // LEN - 1, gs=gs, own=False, **other)
        got, gs = tie((got, gs))
        g = g + got
        g = g + along(g, 8, 2)
        for bit in range(4, bits):
            g = g + along(g, 1 << bit)
        parts = call(
            "finish_qkv", finish_qkv, ins=(g, along(g, 1)), outs=[((width, local), F32)] * 3
        )
        return (step + 1, gs, *parts)

    once = jnp.minimum(lengths[0], 1)
    empty = jnp.zeros((width, local), F32)
    _, gs, gq, gk, gv = lax.cond(
        once > 0, attention_and_sums, lambda c: c,
        (jnp.zeros_like(once), gs, empty, empty, empty),
    )
    grads, gs, gq = tie((grads, gs, gq))
    gu, gi, go, *vec = finish_ff(*grads)
    return (
        new_state, gs, gq, gk, gv, go, vec[0], vec[1], gi, gu, vec[2], vec[3], vec[4]
    )


def solution(mesh):
    rows, columns, parts = P("dp", None), P(None, "mp"), P("mp", None)
    return jax.shard_map(
        functools.partial(shards, mesh.shape["dp"]),
        mesh=mesh,
        in_specs=(
            rows, P("dp"), P("dp"), columns, columns, columns, parts, P(), P(), columns,
            parts, P(), P(), P(), rows
        ),
        out_specs=(
            rows, rows, columns, columns, columns, parts, P(), P(), columns, parts, P(), P(),
            P()
        ),
        check_vma=False,
    )
```

profile of v0, /device:TPU:0, one launch (start us, length us, event | category | flops | bytes accessed | tf_op | source)
XLA Modules:
  0.0 278.2 jit_solution(4668090520957433063)
XLA Ops:
  7.2 0.0 all-reduce.3.cloned.1.call-start
  7.2 0.7 and_xor_fusion.place
  7.9 2.2 pack_qkv.1
  10.1 2.9 %collective-permute-start.5 = (f32[128,768]{1,0:T(8,128)}, f32[128,768]{1,0:T(8,128)}, u32[]{:S(2)}, u32[]{:S(2)}) collective-permute-start(f32[128,768]{1,0:T(8,128)} %pack_qkv.1), channel_id=1, source_target_pairs={{0,1},{1,0},{2,3},{3,2},{4,5},{5,4},{6,7},{7,6},{8,9},{9,8},{10,11... | collective-permute-start | bytes 1179656 | tf_op jit(solution)/shard_map/ppermute | solution.py:698
  13.1 3.2 %embed.1.x_in = bf16[2048,512]{1,0:T(8,128)(2,1)S(1)} custom-call(bf16[2048,512]{1,0:T(8,128)(2,1)} %state.3, f32[1024,512]{1,0:T(8,128)} %constant.20.clone.timing), custom_call_target="tpu_custom_call" | custom-call | tf_op jit(solution)/shard_map/embed/pallas_call | solution.py:601
  16.2 0.0 copy-start.11
  16.2 0.0 copy-start.13
  16.2 0.0 copy-start.14
  16.3 0.0 copy-start.1
  16.3 0.0 copy-start.2
  16.3 0.0 copy-start.3
  16.3 2.7 pack_ff.1
  19.0 0.0 collective-permute-start.7
  19.0 1.3 stack.26.vectors
  20.3 8.9 %attention_forward.4 = (bf16[8,1024,1024]{2,1,0:T(8,128)(2,1)}, bf16[256,2048]{1,0:T(8,128)(2,1)}, f32[8,1,1024]{2,1,0:T(1,128)}) custom-call(s32[2]{0:T(128)} %lengths.7, bf16[2048,512]{1,0:T(8,128)(2,1)S(1)} %embed.1.x_in, bf16[512,256]{1,0:T(8,128)(2,1)S(1)} %copy-done.1, bf16[512,256]{1,0:T(8,128)(2,1)S(1)} %copy-done.2, bf16[512,256]{1,0:T(8,128)(2,1)S(1)} %copy-done.3), custom_call_target="tpu_custom_call" | custom-call | flops 4294967296 | bytes 8388608 | tf_op jit(solution)/shard_map/attention_forward/pallas_call | solution.py:153
  29.2 0.0 collective-permute-done.5.refs_0_
  29.3 0.0 collective-permute-start.11
  29.3 2.1 collective-permute-start.6
  31.4 8.9 %attention_forward.5 = (bf16[8,1024,1024]{2,1,0:T(8,128)(2,1)}, bf16[256,2048]{1,0:T(8,128)(2,1)}, f32[8,1,1024]{2,1,0:T(1,128)}) custom-call(s32[2]{0:T(128)} %lengths.7, bf16[2048,512]{1,0:T(8,128)(2,1)S(1)} %embed.1.x_in, bf16[512,256]{1,0:T(8,128)(2,1)S(1)} %copy-done.1, ...), custom_call_target="tpu_custom_call", output_to_operand_aliasing={{0}: (5, {}), {1}: (6, {}), {2}: (7, {})} | custom-call | flops 4294967296 | bytes 8388608 | tf_op jit(solution)/shard_map/attention_forward/pallas_call | solution.py:153
  40.3 1.1 collective-permute-done.6.refs_1_
  41.4 0.0 collective-permute-start.12
  41.4 1.7 collective-permute-start.9
  43.1 1.5 collective-permute-start.10
  44.6 0.0 collective-permute-start.8
  44.7 2.3 unpack_qkv.1
  47.0 9.6 %attention_forward.6 = (bf16[8,1024,1024]{2,1,0:T(8,128)(2,1)}, bf16[256,2048]{1,0:T(8,128)(2,1)}, f32[8,1,1024]{2,1,0:T(1,128)}) custom-call(s32[2]{0:T(128)} %lengths.7, bf16[2048,512]{1,0:T(8,128)(2,1)S(1)} %embed.1.x_in, bf16[512,256]{1,0:T(8,128)(2,1)} %get-tuple-element.166.wq, bf16[512,256]{1,0:T(8,128)(2,1)} %get-tuple-element.167.wk, ...), custom_call_target="tpu_custom_call" | custom-call | flops 4294967296 | bytes 8388608 | tf_op jit(solution)/shard_map/attention_forward/pallas_call | solution.py:153
  56.6 0.8 collective-permute-done.10.refs_0_
  57.4 1.2 collective-permute-done.9.refs_1_
  58.7 0.5 collective-permute-start.14
  59.2 1.7 collective-permute-start.15
  60.9 9.3 %attention_forward.7 = (bf16[8,1024,1024]{2,1,0:T(8,128)(2,1)}, bf16[256,2048]{1,0:T(8,128)(2,1)}, f32[8,1,1024]{2,1,0:T(1,128)}) custom-call(s32[2]{0:T(128)} %lengths.7, bf16[2048,512]{1,0:T(8,128)(2,1)S(1)} %embed.1.x_in, bf16[512,256]{1,0:T(8,128)(2,1)} %get-tuple-element.166.wq, ...), custom_call_target="tpu_custom_call", output_to_operand_aliasing={{0}: (5, {}), {1}: (6, {}), {2}: (7, {})} | custom-call | flops 4294967296 | bytes 8388608 | tf_op jit(solution)/shard_map/attention_forward/pallas_call | solution.py:153
  70.2 0.0 collective-permute-done.8.refs_2_
  70.2 2.9 %unpack_inner.1 = (bf16[256,512]{1,0:T(8,128)(2,1)}, bf16[512,1024]{1,0:T(8,128)(2,1)}) custom-call(s32[5]{0:T(128)S(1)} %and_xor_fusion.place, f32[320,512]{1,0:T(8,128)} %copy-done.5, f32[320,512]{1,0:T(8,128)} %collective-permute-done.9.refs_1_, f32[320,512]{1,0:T(8,128)} %collective-permute-done.8.refs_2_, f32[320,512]{1,0:T(8,128)} %collective-permute-done.13.refs_3_), custom_call_target="tpu_custom_call" | custom-call | tf_op jit(solution)/shard_map/unpack_inner/pallas_call | solution.py:548
  73.1 2.1 collective-permute-done.16.refs_3_
  75.2 0.8 copy-done.7
  76.0 2.6 unpack_outer.1.wu_b
  78.7 57.2 %middle.1 = (f32[2048,512]{1,0:T(8,128)}, f32[2048,512]{1,0:T(8,128)}, f32[256,2048]{1,0:T(8,128)}, f32[256,2048]{1,0:T(8,128)}, f32[8,1,1024]{2,1,0:T(1,128)S(1...) custom-call(bf16[2048,512]{1,0:T(8,128)(2,1)} %state.3, ...), custom_call_target="tpu_custom_call" | custom-call | flops 24696061952 | bytes 20971520 | tf_op jit(solution)/shard_map/middle/pallas_call | solution.py:341
  135.8 0.0 copy-start.12
  135.8 0.0 copy-start.8
  135.8 0.0 all-reduce.3.cloned.1.call-update
  135.9 0.6 copy-done.12
  136.5 0.3 copy-done.8
  136.8 118.1 %conditional.1 = (f32[2048,512]{1,0:T(8,128)}, f32[512,256]{1,0:T(8,128)}, f32[512,256]{1,0:T(8,128)}, f32[512,256]{1,0:T(8,128)}) conditional(s32[]{:T(128)} %bitcast.6, f32[2048,512]{1,0:T(8,128)} %get-tuple-element.196, (s32[5]{0:T(128)S(1)}, bf16[8,1024,1024]{2,1,0:T(8,128)(2,1)}, f32[256,2048]{1,0:T(8,128)}, f32[8,1,1024]{2,1,0:T(1,128)S(1)}, ...), branch_computations={%region_3.0_spmd, %region_4.0_spmd} | conditional | flops 68720263168 | bytes 33557784 | solution.py:778
  136.8 0.6 slice.6.core
  137.4 28.5 %attention_backward_own.1 = (f32[2048,512]{1,0:T(8,128)}, f32[256,768]{1,0:T(8,128)}, f32[256,768]{1,0:T(8,128)}) custom-call(s32[1]{0:T(128)} %slice.6.core, bf16[8,1024,1024]{2,1,0:T(8,128)(2,1)} %get-tuple-element.35.e_in, f32[256,2048]{1,0:T(8,128)} %get-tuple-element.36.do_in, ...), custom_call_target="tpu_custom_call", output_to_operand_aliasing={{0}: (8, {})} | custom-call | flops 34359738368 | bytes 1000 | tf_op jit(solution)/shard_map/cond/branch_1_fun/attention_backward_own/pallas_call | solution.py:504
  165.9 0.2 collective-permute-start
  166.1 2.4 collective-permute-done
  168.5 1.2 add.14
  169.7 1.8 collective-permute-start.1
  171.5 15.0 %attention_backward_other.2.gs_in = f32[2048,512]{1,0:T(8,128)} custom-call(s32[1]{0:T(128)} %slice.6.core, bf16[8,1024,1024]{2,1,0:T(8,128)(2,1)} %get-tuple-element.47.e_in, f32[256,2048]{1,0:T(8,128)} %get-tuple-element.48.do_in, f32[8,1,1024]{2,1,0:T(1,128)S(1)} %get-tuple-element.49.dl_in, ...), custom_call_target="tpu_custom_call", output_to_operand_aliasing={{}: (8, {})} | custom-call | flops 17179869184 | bytes 1000 | tf_op jit(solution)/shard_map/cond/branch_1_fun/attention_backward_other/pallas_call | solution.py:504
  186.6 1.2 add.15
  187.8 1.6 collective-permute-start.2
  189.4 15.2 %attention_backward_other.3 = f32[2048,512]{1,0:T(8,128)} custom-call(s32[1]{0:T(128)} %slice.6.core, bf16[8,1024,1024]{2,1,0:T(8,128)(2,1)} %get-tuple-element.47.e_in, f32[256,2048]{1,0:T(8,128)} %get-tuple-element.48.do_in, f32[8,1,1024]{2,1,0:T(1,128)S(1)} %get-tuple-element.49.dl_in, ...), custom_call_target="tpu_custom_call", output_to_operand_aliasing={{}: (8, {})} | custom-call | flops 17179869184 | bytes 1000 | tf_op jit(solution)/shard_map/cond/branch_1_fun/attention_backward_other/pallas_call | solution.py:504
  204.6 9.7 %collective-permute-done.2 = f32[256,768]{1,0:T(8,128)S(1)} collective-permute-done((f32[256,768]{1,0:T(8,128)S(1)}, f32[256,768]{1,0:T(8,128)S(1)}, u32[]{:S(2)}, u32[]{:S(2)}) %collective-permute-start.2) | collective-permute-done | bytes 786464 | tf_op jit(solution)/shard_map/cond/branch_1_fun/ppermute | solution.py:701
  214.3 0.1 add.16
  214.3 3.1 %collective-permute-start.3 = (f32[256,768]{1,0:T(8,128)S(1)}, f32[256,768]{1,0:T(8,128)S(1)}, u32[]{:S(2)}, u32[]{:S(2)}) collective-permute-start(f32[256,768]{1,0:T(8,128)S(1)} %add.16), channel_id=1, source_target_pairs={{0,16},{2,6},{4,20},{6,2},{8,24},{10,14},{12,28},{14,10},{16,0},{1... | collective-permute-start | bytes 2359304 | tf_op jit(solution)/shard_map/cond/branch_1_fun/ppermute | solution.py:701
  217.5 31.5 %collective-permute-done.3 = f32[256,768]{1,0:T(8,128)S(1)} collective-permute-done((f32[256,768]{1,0:T(8,128)S(1)}, f32[256,768]{1,0:T(8,128)S(1)}, u32[]{:S(2)}, u32[]{:S(2)}) %collective-permute-start.3) | collective-permute-done | bytes 786464 | tf_op jit(solution)/shard_map/cond/branch_1_fun/ppermute | solution.py:701
  248.9 0.1 add.17.refs_0_
  249.0 0.1 collective-permute-start.4
  249.1 2.3 collective-permute-done.4.refs_1_
  251.4 0.9 copy-done.4
  252.3 2.6 finish_qkv.1
  254.9 11.1 %all-reduce.3.cloned.1.call-done = (f32[1024,512]{1,0:T(8,128)}, f32[512,1024]{1,0:T(8,128)}, f32[264,512]{1,0:T(8,128)}) async-done(((f32[1024,512]{1,0:T(8,128)}, f32[512,1024]{1,0:T(8,128)}, f32[264,512]{1,0:T(8,128)}), (f32[1024,512]{1,0:T(8,128)}, f32[512,1024]{1,0:T(8,128)}, f32[264,512]{1,0:T(8,128)})) %all-reduce.3.cloned.1.call-update) | async-done | bytes 4734992 | tf_op jit(solution)/shard_map/psum | solution.py:749
  266.0 5.1 %finish_ff.1 = (f32[1024,512]{1,0:T(8,128)}, f32[512,1024]{1,0:T(8,128)}, f32[256,512]{1,0:T(8,128)}, f32[512]{0:T(512)}, f32[512]{0:T(512)}, /*index=5*/f32[512]{0:T(512)}, f32[512]{0:T(512)}, f32[512]{0:T(512)}) custom-call(f32[1024,512]{1,0:T(8,128)} %get-tuple-element.209.gu_in, f32[512,1024]{1,0:T(8,128)} %get-tuple-element.210.gi_in, ...), custom_call_target="tpu_custom_call" | custom-call | tf_op jit(solution)/shard_map/finish_ff/pallas_call | solution.py:664
  (27 shorter events, 0.1 us)
Async XLA Ops:
  7.2 258.9 %all-reduce.3.cloned.1.call-start = ((), (), s32[]{:S(2)}) async-start(), calls=%async_computation | async-start | bytes 9469952 | tf_op jit(solution)/shard_map/psum | solution.py:749
  10.1 19.1 %collective-permute-start.5 = (f32[128,768]{1,0:T(8,128)}, f32[128,768]{1,0:T(8,128)}, u32[]{:S(2)}, u32[]{:S(2)}) collective-permute-start(f32[128,768]{1,0:T(8,128)} %pack_qkv.1), channel_id=1, source_target_pairs={{0,1},{1,0},{2,3},{3,2},{4,5},{5,4},{6,7},{7,6},{8,9},{9,8},{10,11... | collective-permute-start | bytes 1179656 | tf_op jit(solution)/shard_map/ppermute | solution.py:698
  16.2 2.7 copy-start.11
  16.2 2.7 copy-start.13
  16.2 2.7 copy-start.14
  16.3 4.0 %copy-start.1 = (bf16[512,256]{1,0:T(8,128)(2,1)S(1)}, bf16[512,256]{1,0:T(8,128)(2,1)}, u32[]{:S(2)}) copy-start(bf16[512,256]{1,0:T(8,128)(2,1)} %wq.3) | copy-start | bytes 786436
  16.3 4.0 %copy-start.2 = (bf16[512,256]{1,0:T(8,128)(2,1)S(1)}, bf16[512,256]{1,0:T(8,128)(2,1)}, u32[]{:S(2)}) copy-start(bf16[512,256]{1,0:T(8,128)(2,1)} %wk.3) | copy-start | bytes 786436
  16.3 4.0 %copy-start.3 = (bf16[512,256]{1,0:T(8,128)(2,1)S(1)}, bf16[512,256]{1,0:T(8,128)(2,1)}, u32[]{:S(2)}) copy-start(bf16[512,256]{1,0:T(8,128)(2,1)} %wv.3) | copy-start | bytes 786436
  19.0 21.3 %collective-permute-start.7 = (f32[320,512]{1,0:T(8,128)}, f32[320,512]{1,0:T(8,128)S(1)}, u32[]{:S(2)}, u32[]{:S(2)}) collective-permute-start(f32[320,512]{1,0:T(8,128)} %get-tuple-element.155), channel_id=1, source_target_pairs={{0,1},{1,0},{2,3},{3,2},{4,5},{5,4},{6,7},{7,6},{8,9},{9,8},{10,11... | collective-permute-start | bytes 1966088 | tf_op jit(solution)/shard_map/ppermute | solution.py:698
  29.3 15.4 %collective-permute-start.11 = (f32[128,768]{1,0:T(8,128)}, f32[128,768]{1,0:T(8,128)}, u32[]{:S(2)}, u32[]{:S(2)}) collective-permute-start(f32[128,768]{1,0:T(8,128)} %collective-permute-done.5.refs_0_), channel_id=1, source_target_pairs={{0,2},{2,0},{4,6},{6,4},{8,10},{10,8},{12,14},{14,12},{16,18},{18,... | collective-permute-start | bytes 1179656 | tf_op jit(solution)/shard_map/ppermute | solution.py:701
  29.3 12.1 %collective-permute-start.6 = (f32[128,768]{1,0:T(8,128)}, f32[128,768]{1,0:T(8,128)}, u32[]{:S(2)}, u32[]{:S(2)}) collective-permute-start(f32[128,768]{1,0:T(8,128)} %collective-permute-done.5.refs_0_), channel_id=1, source_target_pairs={{0,4},{2,6},{4,0},{6,2},{8,12},{10,14},{12,8},{14,10},{16,20},{18,... | collective-permute-start | bytes 1179656 | tf_op jit(solution)/shard_map/ppermute | solution.py:701
  40.3 16.4 %copy-start.5 = (f32[320,512]{1,0:T(8,128)}, f32[320,512]{1,0:T(8,128)S(1)}, u32[]{:S(2)}) copy-start(f32[320,512]{1,0:T(8,128)S(1)} %collective-permute-done.7.refs_0_) | copy-start | bytes 1966084
  41.4 3.3 %collective-permute-start.12 = (f32[128,768]{1,0:T(8,128)}, f32[128,768]{1,0:T(8,128)}, u32[]{:S(2)}, u32[]{:S(2)}) collective-permute-start(f32[128,768]{1,0:T(8,128)} %collective-permute-done.6.refs_1_), channel_id=1, source_target_pairs={{0,2},{2,0},{4,6},{6,4},{8,10},{10,8},{12,14},{14,12},{16,18},{18,... | collective-permute-start | bytes 1179656 | tf_op jit(solution)/shard_map/ppermute | solution.py:701
  41.4 17.3 %collective-permute-start.9 = (f32[320,512]{1,0:T(8,128)S(1)}, f32[320,512]{1,0:T(8,128)}, u32[]{:S(2)}, u32[]{:S(2)}) collective-permute-start(f32[320,512]{1,0:T(8,128)S(1)} %collective-permute-done.7.refs_0_), channel_id=1, source_target_pairs={{0,4},{2,6},{4,0},{6,2},{8,12},{10,14},{12,8},{14,10},{16,20},{18,... | collective-permute-start | bytes 1966088 | tf_op jit(solution)/shard_map/ppermute | solution.py:701
  43.1 14.3 %collective-permute-start.10 = (f32[256,512]{1,0:T(8,128)}, f32[256,512]{1,0:T(8,128)S(1)}, u32[]{:S(2)}, u32[]{:S(2)}) collective-permute-start(f32[256,512]{1,0:T(8,128)} %get-tuple-element.164), channel_id=1, source_target_pairs={{0,1},{1,0},{2,3},{3,2},{4,5},{5,4},{6,7},{7,6},{8,9},{9,8},{10,11... | collective-permute-start | bytes 1572872 | tf_op jit(solution)/shard_map/ppermute | solution.py:698
  44.6 25.6 %collective-permute-start.8 = (f32[320,512]{1,0:T(8,128)S(1)}, f32[320,512]{1,0:T(8,128)}, u32[]{:S(2)}, u32[]{:S(2)}) collective-permute-start(f32[320,512]{1,0:T(8,128)S(1)} %collective-permute-done.7.refs_0_), channel_id=1, source_target_pairs={{0,2},{2,0},{4,6},{6,4},{8,10},{10,8},{12,14},{14,12},{16,18},{18,... | collective-permute-start | bytes 1966088 | tf_op jit(solution)/shard_map/ppermute | solution.py:701
  57.4 12.8 %copy-start.6 = (f32[256,512]{1,0:T(8,128)}, f32[256,512]{1,0:T(8,128)S(1)}, u32[]{:S(2)}) copy-start(f32[256,512]{1,0:T(8,128)S(1)} %collective-permute-done.10.refs_0_) | copy-start | bytes 1572868
  58.6 11.6 %collective-permute-start.13 = (f32[320,512]{1,0:T(8,128)}, f32[320,512]{1,0:T(8,128)}, u32[]{:S(2)}, u32[]{:S(2)}) collective-permute-start(f32[320,512]{1,0:T(8,128)} %collective-permute-done.9.refs_1_), channel_id=1, source_target_pairs={{0,2},{2,0},{4,6},{6,4},{8,10},{10,8},{12,14},{14,12},{16,18},{18,... | collective-permute-start | bytes 1966088 | tf_op jit(solution)/shard_map/ppermute | solution.py:701
  58.7 11.6 %collective-permute-start.14 = (f32[256,512]{1,0:T(8,128)S(1)}, f32[256,512]{1,0:T(8,128)}, u32[]{:S(2)}, u32[]{:S(2)}) collective-permute-start(f32[256,512]{1,0:T(8,128)S(1)} %collective-permute-done.10.refs_0_), channel_id=1, source_target_pairs={{0,2},{2,0},{4,6},{6,4},{8,10},{10,8},{12,14},{14,12},{16,18},{18,... | collective-permute-start | bytes 1572872 | tf_op jit(solution)/shard_map/ppermute | solution.py:701
  59.2 14.0 %collective-permute-start.15 = (f32[256,512]{1,0:T(8,128)S(1)}, f32[256,512]{1,0:T(8,128)}, u32[]{:S(2)}, u32[]{:S(2)}) collective-permute-start(f32[256,512]{1,0:T(8,128)S(1)} %collective-permute-done.10.refs_0_), channel_id=1, source_target_pairs={{0,4},{2,6},{4,0},{6,2},{8,12},{10,14},{12,8},{14,10},{16,20},{18,... | collective-permute-start | bytes 1572872 | tf_op jit(solution)/shard_map/ppermute | solution.py:701
  73.1 2.1 collective-permute-start.16
  75.2 0.8 copy-start.7
  135.8 0.7 copy-start.12
  135.8 1.0 copy-start.8
  165.9 5.6 %copy-start.9 = (bf16[512,256]{1,0:T(8,128)(2,1)S(1)}, bf16[512,256]{1,0:T(8,128)(2,1)}, u32[]{:S(2)}) copy-start(bf16[512,256]{1,0:T(8,128)(2,1)} %get-tuple-element.51.wk) | copy-start | bytes 786436 | tf_op jit(solution)/shard_map/cond
  165.9 5.6 %copy-start.10 = (bf16[512,256]{1,0:T(8,128)(2,1)S(1)}, bf16[512,256]{1,0:T(8,128)(2,1)}, u32[]{:S(2)}) copy-start(bf16[512,256]{1,0:T(8,128)(2,1)} %get-tuple-element.52.wv) | copy-start | bytes 786436 | tf_op jit(solution)/shard_map/cond
  165.9 2.6 collective-permute-start
  169.7 16.9 %collective-permute-start.1 = (f32[256,768]{1,0:T(8,128)S(1)}, f32[256,768]{1,0:T(8,128)}, u32[]{:S(2)}, u32[]{:S(2)}) collective-permute-start(f32[256,768]{1,0:T(8,128)S(1)} %add.14), channel_id=1, source_target_pairs={{0,4},{2,10},{4,0},{6,14},{8,12},{10,2},{12,8},{14,6},{16,20},{18,... | collective-permute-start | bytes 2359304 | tf_op jit(solution)/shard_map/cond/branch_1_fun/ppermute | solution.py:701
  187.8 26.5 %collective-permute-start.2 = (f32[256,768]{1,0:T(8,128)S(1)}, f32[256,768]{1,0:T(8,128)S(1)}, u32[]{:S(2)}, u32[]{:S(2)}) collective-permute-start(f32[256,768]{1,0:T(8,128)S(1)} %add.15), channel_id=1, source_target_pairs={{0,8},{2,18},{4,12},{6,22},{8,0},{10,26},{12,4},{14,30},{16,24},{1... | collective-permute-start | bytes 2359304 | tf_op jit(solution)/shard_map/cond/branch_1_fun/ppermute | solution.py:701
  214.3 34.6 %collective-permute-start.3 = (f32[256,768]{1,0:T(8,128)S(1)}, f32[256,768]{1,0:T(8,128)S(1)}, u32[]{:S(2)}, u32[]{:S(2)}) collective-permute-start(f32[256,768]{1,0:T(8,128)S(1)} %add.16), channel_id=1, source_target_pairs={{0,16},{2,6},{4,20},{6,2},{8,24},{10,14},{12,28},{14,10},{16,0},{1... | collective-permute-start | bytes 2359304 | tf_op jit(solution)/shard_map/cond/branch_1_fun/ppermute | solution.py:701
  249.0 2.4 copy-start
  249.0 2.4 collective-permute-start.4
  251.4 0.9 copy-start.4
Sparse Core Ops, SparseCore 0:
  136.0 130.0 all-reduce.2
where the time goes:
time: 279 us; the launch traced here: 278 us
  Pallas kernels  176 us (63%)
  waiting for transfers between devices  62.2 us (22%)
  starting transfers between devices  17.5 us (6%)
  between operations  14.4 us (5%)
  local copies, waits for them, and re-layouts  4.57 us (2%)
  other arithmetic  3.3 us (1%)
    pallas_call x3, Pallas kernels, attention_backward(): pl.pallas_call(functools.partial(attention_backward_kernel, heads=heads,...  58.7 us
    pallas_call x1, Pallas kernels, middle(): pl.pallas_call(functools.partial(middle_kernel, heads=heads), grid=(rows...  57.2 us
    ppermute x14, waiting for transfers between devices, along(): return lax.ppermute(v, 'dp', flipped(dp, even, odd or even))  50.2 us
    pallas_call x4, Pallas kernels, attention_forward(): pl.pallas_call(functools.partial(attention_forward_kernel, seq, heads=hea...  36.8 us
    ppermute x14, starting transfers between devices, along(): return lax.ppermute(v, 'dp', flipped(dp, even, odd or even))  13 us
    psum x1, waiting for transfers between devices, shards(): grads = lax.psum(tuple(grads), 'dp')  11.1 us
    pallas_call x4, Pallas kernels, local_call(): pl.pallas_call(functools.partial(local_kernel, fn, len(ins)), in_specs=[p...  10.4 us
  transfers between devices with their start and end apart: 18, of which 9 were waited for; matrix products, arithmetic and copies ran while one was open for 2% of the time, Pallas kernels for 39%

commit v1 on v0

--- a/solution.py
+++ b/solution.py
@@ -209,17 +209,29 @@
     return jnp.sum(v.reshape(v.shape[0] // 8, 8, v.shape[1]), axis=0)
 
 
+def unpack(place, inner, outer, wo, wi, wu):
+    width = wi.shape[0]
+    quarter, blocks = width // 4, wi.shape[1] // width
+    for p, ref, more in zip((0, 2, 1, 3), inner, outer):
+        rows = rows_at(place[p], quarter)
+        for n in range(blocks):
+            columns = slice(n * width, (n + 1) * width)
+            wi[rows, columns] = ref[n * quarter : (n + 1) * quarter].astype(BF)
+        wo[rows_at(place[p], wo.shape[0] // 4)] = ref[blocks * quarter :].astype(BF)
+        wu[rows_at(place[p], more.shape[0])] = more[...].astype(BF)
+
+
 def middle_kernel(
-    state, timing, cot, run, mix_a, mix_b, r_a, r_b, wo_a, wo_b, wi_a, wi_b, wu_a, wu_b,
-    vectors, new_state, gs, do_a, do_b, dl_a, dl_b, gu, gi, go, act, slope, inner_low, low1,
-    out_low, att_low, fold, *, heads
+    place, state, timing, cot, run, mix_a, mix_b, r_a, r_b, wo_a, wi_a, wu_a, v0, v1, v2, v3,
+    v4, i0, i1, i2, i3, o0, o1, o2, o3, new_state, gs, do_a, do_b, dl_a, dl_b, gu, gi, go, act,
+    slope, inner_low, low1, out_low, att_low, fold, wo_b, wi_b, wu_b, *, heads
 ):
     t = pl.program_id(0)
     last = pl.num_programs(0) - 1
     tile = state.shape[0]
     size = tile // SUBS
     local = wo_a.shape[0]
-    gain1, bias1, gain2, bias2, halt_w = (vectors[n : n + 1] for n in range(5))
+    gain1, bias1, gain2, bias2, halt_w = (v[...].reshape(1, -1) for v in (v0, v1, v2, v3, v4))
     c0 = math.sqrt(2.0 / math.pi)
     halves = ((wi_a, wu_a), (wi_b, wu_b))
     running_column = jnp.broadcast_to(run[0].astype(F32), (8, tile)).T[:, 0:1]
@@ -228,6 +240,7 @@
     def _():
         for ref in (gu, gi, go, fold):
             ref[...] = jnp.zeros(ref.shape, F32)
+        unpack(place, (i0, i1, i2, i3), (o0, o1, o2, o3), wo_b, wi_b, wu_b)
 
     def first_norm(k):
         rows = slice(k * size, (k + 1) * size)
@@ -328,8 +341,8 @@
             go[local + n : local + n + 1] = jnp.sum(fold[n], axis=0, keepdims=True)
 
 
-def middle(state, timing, cot, run, mix_a, mix_b, r_a, r_b, wo_a, wo_b, wi_a, wi_b, wu_a,
-           wu_b, vectors):
+def middle(place, state, timing, cot, run, mix_a, mix_b, r_a, r_b, wo_a, wi_a, wu_a, vectors,
+           inner, outer):
     rows, width = state.shape
     local, ff = wo_a.shape[0], wi_a.shape[1]
     heads = local // HEAD
@@ -342,6 +355,7 @@
         functools.partial(middle_kernel, heads=heads),
         grid=(rows // tile,),
         in_specs=[
+            pl.BlockSpec(memory_space=pltpu.SMEM),
             by_rows,
             pl.BlockSpec((tile, width), lambda t: (t % per, 0)),
             by_rows,
@@ -351,13 +365,11 @@
             per_head,
             per_head,
             whole((local, width)),
-            whole((local, width)),
-            whole((width, ff)),
             whole((width, ff)),
             whole((ff, width)),
-            whole((ff, width)),
-            whole((8, width)),
-        ],
+        ]
+        + [whole((width,))] * 5
+        + [whole(v.shape) for v in (*inner, *outer)],
         out_specs=[
             by_rows,
             by_rows,
@@ -388,6 +400,9 @@
             pltpu.VMEM((tile, width), BF),
             pltpu.VMEM((tile, width), BF),
             pltpu.VMEM((8, 8, width), F32),
+            pltpu.VMEM((local, width), BF),
+            pltpu.VMEM((width, ff), BF),
+            pltpu.VMEM((ff, width), BF),
         ],
         compiler_params=params(),
         cost_estimate=pl.CostEstimate(
@@ -396,8 +411,8 @@
             transcendentals=2 * rows * ff,
         ),
         name="middle",
-    )(state, timing, cot, run.reshape(rows // tile, 1, tile), mix_a, mix_b, r_a, r_b, wo_a, wo_b, wi_a, wi_b, wu_a, wu_b,
-      vectors)
+    )(place, state, timing, cot, run.reshape(rows // tile, 1, tile), mix_a, mix_b, r_a, r_b,
+      wo_a, wi_a, wu_a, *vectors, *inner, *outer)
 
 
 def attention_backward_kernel(
@@ -573,20 +588,17 @@
     )(place, *ins)
 
 
-def pack_qkv(place, ins, outs):
-    local = ins[0].shape[1]
-    for n, ref in enumerate(ins):
+def pack(place, ins, outs):
+    wq, wk, wv, wo, wi, wu = ins
+    local = wq.shape[1]
+    for n, ref in enumerate((wq, wk, wv)):
         outs[0][:, n * local : (n + 1) * local] = ref[...].astype(F32)
-
-
-def pack_ff(place, ins, outs):
-    wo, wi, wu = ins
     quarter, width = wi.shape[0], wo.shape[1]
     blocks = wi.shape[1] // width
     for n in range(blocks):
-        outs[0][n * quarter : (n + 1) * quarter] = wi[:, n * width : (n + 1) * width].astype(F32)
-    outs[0][blocks * quarter :] = wo[...].astype(F32)
-    outs[1][...] = wu[...].astype(F32)
+        outs[1][n * quarter : (n + 1) * quarter] = wi[:, n * width : (n + 1) * width].astype(F32)
+    outs[1][blocks * quarter :] = wo[...].astype(F32)
+    outs[2][...] = wu[...].astype(F32)
 
 
 def embed_kernel(state, timing, out):
@@ -617,28 +629,11 @@
             out[rows] = ref[:, n * local : (n + 1) * local].astype(BF)
 
 
-def unpack_inner(place, ins, outs):
-    wo, wi = outs
-    width = wi.shape[0]
-    quarter, blocks = width // 4, wi.shape[1] // width
-    for p, ref in zip((0, 2, 1, 3), ins):
-        rows = rows_at(place[p], quarter)
-        for n in range(blocks):
-            wi[rows, n * width : (n + 1) * width] = ref[
-                n * quarter : (n + 1) * quarter
-            ].astype(BF)
-        wo[rows_at(place[p], wo.shape[0] // 4)] = ref[blocks * quarter :].astype(BF)
-
-
-def unpack_outer(place, ins, outs):
-    for p, ref in zip((0, 2, 1, 3), ins):
-        outs[0][rows_at(place[p], ref.shape[0])] = ref[...].astype(BF)
-
-
 def finish_qkv(place, ins, outs):
-    local = outs[0].shape[1]
-    for flip, ref in enumerate(ins):
-        rows = rows_at(jnp.bitwise_xor(place[4], flip), ref.shape[0])
+    few, local = ins[0].shape[0], outs[0].shape[1]
+    for n, ref in enumerate(ins):
+        core, y = jnp.bitwise_xor(place[4], n // 2), jnp.bitwise_xor(place[5], n % 2)
+        rows = rows_at(2 * core + y, few)
         for n, out in enumerate(outs):
             out[rows] = ref[:, n * local : (n + 1) * local]
 
@@ -687,9 +682,10 @@
     local, ff = wq.shape[1], wi.shape[1]
     timing = jnp.asarray(timing_rows(width))
     me = lax.axis_index("dp").astype(jnp.int32)
-    mask = np.array([3, 3, 3, 3, 1], np.int32)
-    flip = np.array([0, 1, 2, 3, 0], np.int32)
-    place = jnp.bitwise_xor(jnp.bitwise_and(me, mask), flip)
+    shift = np.array([0, 0, 0, 0, 0, 1], np.int32)
+    mask = np.array([3, 3, 3, 3, 1, 1], np.int32)
+    flip = np.array([0, 1, 2, 3, 0, 0], np.int32)
+    place = jnp.bitwise_xor(jnp.bitwise_and(jnp.right_shift(me, shift), mask), flip)
     bits = dp.bit_length() - 1
     tie = lax.optimization_barrier
     call = functools.partial(local_call, place=place)
@@ -701,18 +697,16 @@
         return lax.ppermute(v, "dp", flipped(dp, even, odd or even))
 
     quarter = width // 4
-    (chunk_a,) = cut_call("pack_qkv", pack_qkv, place, (wq, wk, wv), [(quarter, 3 * local)])
+    chunk_a, chunk_b, chunk_c = cut_call(
+        "pack", pack, place, (wq, wk, wv, wo, wi, wu),
+        [(quarter, 3 * local), (ff // 4 + local // 4, width), (ff // 4, width)],
+    )
     qkv0 = across(chunk_a)
-    chunk_b, chunk_c = cut_call(
-        "pack_ff", pack_ff, place, (wo, wi, wu),
-        [(ff // 4 + local // 4, width), (ff // 4, width)],
-    )
     x = embed(state, timing)
     chunk_b, x = tie((chunk_b, x))
     in0 = across(chunk_b)
-    vectors = jnp.stack([gain1, bias1, gain2, bias2, halt_weight] + [gain1] * 3)
     fwd = attention_forward(0, lengths, x, wq, wk, wv)
-    qkv0, chunk_c, vectors, fwd = tie((qkv0, chunk_c, vectors, fwd))
+    qkv0, chunk_c, fwd = tie((qkv0, chunk_c, fwd))
     qkv1 = along(qkv0, 2)
     out0 = across(chunk_c)
     fwd = attention_forward(1, lengths, x, wq, wk, wv, fwd)
@@ -729,26 +723,18 @@
     out1 = along(out0, 2)
     out2 = along(out0, 1)
     fwd2 = attention_forward(1, lengths, x, wq2, wk2, wv2, fwd2)
-    in2, in3, out2, fwd2 = tie((in2, in3, out2, fwd2))
-    wo2, wi2 = call(
-        "unpack_inner", unpack_inner, ins=(in0, in1, in2, in3),
-        outs=[((local, width), BF), ((width, ff), BF)],
-    )
-    out1, wo2, wi2 = tie((out1, wo2, wi2))
+    in2, in3, out1, out2, fwd2 = tie((in2, in3, out1, out2, fwd2))
     out3 = along(out1, 1)
-    (wu2,) = call(
-        "unpack_outer", unpack_outer, ins=(out0, out1, out2, out3), outs=[((ff, width), BF)]
-    )
     e_a, mix_a, r_a = fwd
     e_b, mix_b, r_b = fwd2
     new_state, gs, do_a, do_b, dl_a, dl_b, *grads = middle(
-        state, timing, cotangent, halt_mask, mix_a, mix_b, r_a, r_b, wo, wo2, wi, wi2, wu, wu2,
-        vectors
+        place, state, timing, cotangent, halt_mask, mix_a, mix_b, r_a, r_b, wo, wi, wu,
+        (gain1, bias1, gain2, bias2, halt_weight), (in0, in1, in2, in3), (out0, out1, out2, out3)
     )
 
     grads = lax.psum(tuple(grads), "dp")
-    own = dict(core=place[4:], e=e_a, do=do_a, dl=dl_a, x=x, wq=wq, wk=wk, wv=wv)
-    other = dict(core=place[4:], e=e_b, do=do_b, dl=dl_b, x=x, wq=wq2, wk=wk2, wv=wv2)
+    own = dict(core=place[4:5], e=e_a, do=do_a, dl=dl_a, x=x, wq=wq, wk=wk, wv=wv)
+    other = dict(core=place[4:5], e=e_b, do=do_b, dl=dl_b, x=x, wq=wq2, wk=wk2, wv=wv2)
 
     def attention_and_sums(carry):
         step, gs, *_ = carry
@@ -756,20 +742,24 @@
         gs, keep, send = back(0, rows // LEN, gs=gs, own=True, **own)
         g = keep + along(send, 1)
         g, gs = tie((g, gs))
-        got = along(g, 2, 4)
+        few = g.shape[0] // 2
+        y = place[5]
+        got = along(lax.dynamic_slice_in_dim(g, (1 - y) * few, few), 2)
         (gs,) = back(0, 1, gs=gs, own=False, **other)
         got, gs = tie((got, gs))
-        g = g + got
+        g = lax.dynamic_slice_in_dim(g, y * few, few) + got
         g, gs = tie((g, gs))
         got = along(g, 4, 8)
         (gs,) = back(1, rows // LEN - 1, gs=gs, own=False, **other)
         got, gs = tie((got, gs))
         g = g + got
-        g = g + along(g, 8, 2)
+        g = g + along(g, 8, 4)
         for bit in range(4, bits):
             g = g + along(g, 1 << bit)
+        got = along(g, 2)
         parts = call(
-            "finish_qkv", finish_qkv, ins=(g, along(g, 1)), outs=[((width, local), F32)] * 3
+            "finish_qkv", finish_qkv, ins=(g, got, along(g, 1), along(got, 1)),
+            outs=[((width, local), F32)] * 3,
         )
         return (step + 1, gs, *parts)
 

time: 279 us -> 270 us (0.968)
  Pallas kernels: 176 us -> 169 us
    ppermute x14 -> x16, waiting for transfers between devices: 50.2 us -> 39.9 us  [along(): return lax.ppermute(v, 'dp', flipped(dp, even, odd or even))]
    psum x1, waiting for transfers between devices: 11.1 us -> 18.6 us  [shards(): grads = lax.psum(tuple(grads), 'dp')]
    pallas_call x4 -> x2, Pallas kernels: 10.4 us -> 4.08 us  [local_call(): pl.pallas_call(functools.partial(local_kernel, fn, len(ins)), in_specs=[p...]
    ppermute x14 -> x16, starting transfers between devices: 13 us -> 13.5 us  [along(): return lax.ppermute(v, 'dp', flipped(dp, even, odd or even))]
  transfers between devices with their start and end apart: 18 -> 20, of which waited for: 9 -> 11; matrix products, arithmetic and copies ran while one was open for 2% -> 1% of each run, Pallas kernels for 39% -> 38%
where the time goes in v1:
time: 270 us
  Pallas kernels  169 us (63%)
  waiting for transfers between devices  60.3 us (22%)
  starting transfers between devices  18.2 us (7%)
  between operations  14.4 us (5%)
  local copies, waits for them, and re-layouts  4.5 us (2%)
    pallas_call x3, Pallas kernels, attention_backward(): pl.pallas_call(functools.partial(attention_backward_kernel, heads=heads,...  59 us
    pallas_call x1, Pallas kernels, middle(): pl.pallas_call(functools.partial(middle_kernel, heads=heads), grid=(rows...  58.6 us
    ppermute x16, waiting for transfers between devices, along(): return lax.ppermute(v, 'dp', flipped(dp, even, odd or even))  39.9 us
    pallas_call x4, Pallas kernels, attention_forward(): pl.pallas_call(functools.partial(attention_forward_kernel, seq, heads=hea...  35.8 us
    psum x1, waiting for transfers between devices, shards(): grads = lax.psum(tuple(grads), 'dp')  18.6 us
    ppermute x16, starting transfers between devices, along(): return lax.ppermute(v, 'dp', flipped(dp, even, odd or even))  13.5 us
  transfers between devices with their start and end apart: 20, of which 11 were waited for; matrix products, arithmetic and copies ran while one was open for 1% of the time, Pallas kernels for 38%

profile of v1, /device:TPU:0, one launch (start us, length us, event | category | flops | bytes accessed | tf_op | source)
XLA Modules:
  0.0 269.7 jit_solution(8264137395422813833)
XLA Ops:
  7.2 0.0 all-reduce.3.cloned.1.call-start
  7.2 0.7 and_xor_fusion.place
  7.9 2.9 %pack.1 = (f32[128,768]{1,0:T(8,128)}, f32[320,512]{1,0:T(8,128)}, f32[256,512]{1,0:T(8,128)}) custom-call(s32[6]{0:T(128)S(1)} %and_xor_fusion.place, bf16[512,256]{1,0:T(8,128)(2,1)} %wq.3, bf16[512,256]{1,0:T(8,128)(2,1)} %wk.3, bf16[512,256]{1,0:T(8,128)(2,1)} %wv.3, bf16[256,512]{1,0:T(8,128)(2,1)} %wo_a.1, bf16[512,1024]{1,0:T(8,128)(2,1)} %wi_a.1, ...), custom_call_target="tpu_custom_call" | custom-call | tf_op jit(solution)/shard_map/pack/pallas_call | solution.py:575
  10.8 3.0 %collective-permute-start.7 = (f32[128,768]{1,0:T(8,128)}, f32[128,768]{1,0:T(8,128)S(1)}, u32[]{:S(2)}, u32[]{:S(2)}) collective-permute-start(f32[128,768]{1,0:T(8,128)} %get-tuple-element.144), channel_id=1, source_target_pairs={{0,1},{1,0},{2,3},{3,2},{4,5},{5,4},{6,7},{7,6},{8,9},{9,8},{10,11... | collective-permute-start | bytes 1179656 | tf_op jit(solution)/shard_map/ppermute | solution.py:694
  13.8 3.2 %embed.1.x_in = bf16[2048,512]{1,0:T(8,128)(2,1)S(1)} custom-call(bf16[2048,512]{1,0:T(8,128)(2,1)} %state.3, f32[1024,512]{1,0:T(8,128)} %constant.33.clone.timing), custom_call_target="tpu_custom_call" | custom-call | tf_op jit(solution)/shard_map/embed/pallas_call | solution.py:613
  17.0 0.1 collective-permute-start.9
  17.1 8.9 %attention_forward.4 = (bf16[8,1024,1024]{2,1,0:T(8,128)(2,1)}, bf16[256,2048]{1,0:T(8,128)(2,1)}, f32[8,1,1024]{2,1,0:T(1,128)}) custom-call(s32[2]{0:T(128)} %lengths.7, bf16[2048,512]{1,0:T(8,128)(2,1)S(1)} %embed.1.x_in, bf16[512,256]{1,0:T(8,128)(2,1)S(1)} %copy-done.1, bf16[512,256]{1,0:T(8,128)(2,1)S(1)} %copy-done.2, bf16[512,256]{1,0:T(8,128)(2,1)S(1)} %copy-done.3), custom_call_target="tpu_custom_call" | custom-call | flops 4294967296 | bytes 8388608 | tf_op jit(solution)/shard_map/attention_forward/pallas_call | solution.py:153
  26.0 0.0 collective-permute-done.7.refs_0_
  26.0 0.1 collective-permute-start.13
  26.1 2.1 collective-permute-start.8
  28.2 8.9 %attention_forward.5 = (bf16[8,1024,1024]{2,1,0:T(8,128)(2,1)}, bf16[256,2048]{1,0:T(8,128)(2,1)}, f32[8,1,1024]{2,1,0:T(1,128)}) custom-call(s32[2]{0:T(128)} %lengths.7, bf16[2048,512]{1,0:T(8,128)(2,1)S(1)} %embed.1.x_in, bf16[512,256]{1,0:T(8,128)(2,1)S(1)} %copy-done.1, ...), custom_call_target="tpu_custom_call", output_to_operand_aliasing={{0}: (5, {}), {1}: (6, {}), {2}: (7, {})} | custom-call | flops 4294967296 | bytes 8388608 | tf_op jit(solution)/shard_map/attention_forward/pallas_call | solution.py:153
  37.0 0.3 collective-permute-done.9.i0
  37.3 0.7 collective-permute-done.8.refs_1_
  38.0 0.0 collective-permute-start.14
  38.0 1.8 collective-permute-start.11
  39.7 1.5 collective-permute-start.12
  41.2 0.0 collective-permute-start.10
  41.2 0.0 collective-permute-done.13.refs_2_
  41.2 0.0 collective-permute-done.14.refs_3_
  41.2 0.7 copy-done.6
  42.0 1.4 unpack_qkv.1
  43.4 9.1 %attention_forward.6 = (bf16[8,1024,1024]{2,1,0:T(8,128)(2,1)}, bf16[256,2048]{1,0:T(8,128)(2,1)}, f32[8,1,1024]{2,1,0:T(1,128)}) custom-call(s32[2]{0:T(128)} %lengths.7, bf16[2048,512]{1,0:T(8,128)(2,1)S(1)} %embed.1.x_in, bf16[512,256]{1,0:T(8,128)(2,1)S(1)} %get-tuple-element.163.wq, bf16[512,256]{1,0:T(8,128)(2,1)S(1)} %get-tuple-element.164.wk, ...), custom_call_target="tpu_custom_call" | custom-call | flops 4294967296 | bytes 8388608 | tf_op jit(solution)/shard_map/attention_forward/pallas_call | solution.py:153
  52.6 1.5 collective-permute-done.12.o0
  54.1 1.3 collective-permute-done.11.i1
  55.5 0.0 collective-permute-start.15
  55.5 0.5 collective-permute-start.17
  56.0 1.7 collective-permute-start.16
  57.7 8.9 %attention_forward.7 = (bf16[8,1024,1024]{2,1,0:T(8,128)(2,1)}, bf16[256,2048]{1,0:T(8,128)(2,1)}, f32[8,1,1024]{2,1,0:T(1,128)}) custom-call(s32[2]{0:T(128)} %lengths.7, bf16[2048,512]{1,0:T(8,128)(2,1)S(1)} %embed.1.x_in, bf16[512,256]{1,0:T(8,128)(2,1)S(1)} %get-tuple-element.163.wq, ...), custom_call_target="tpu_custom_call", output_to_operand_aliasing={{0}: (5, {}), {1}: (6, {}), {2}: (7, {})} | custom-call | flops 4294967296 | bytes 8388608 | tf_op jit(solution)/shard_map/attention_forward/pallas_call | solution.py:153
  66.6 0.0 collective-permute-done.10.i2
  66.6 0.0 collective-permute-done.17.o2
  66.6 3.5 %collective-permute-done.16.o1 = f32[256,512]{1,0:T(8,128)} collective-permute-done((f32[256,512]{1,0:T(8,128)}, f32[256,512]{1,0:T(8,128)}, u32[]{:S(2)}, u32[]{:S(2)}) %collective-permute-start.16) | collective-permute-done | bytes 524320 | tf_op jit(solution)/shard_map/ppermute | solution.py:697
  70.1 0.0 collective-permute-done.15.i3
  70.1 0.0 collective-permute-start.18
  70.1 2.1 collective-permute-done.18.o3
  72.2 0.8 copy-done.13
  73.0 58.6 %middle.1 = (f32[2048,512]{1,0:T(8,128)}, f32[2048,512]{1,0:T(8,128)}, f32[256,2048]{1,0:T(8,128)}, f32[256,2048]{1,0:T(8,128)}, f32[8,1,1024]{2,1,0:T(1,128)S(1...) custom-call(s32[6]{0:T(128)S(1)} %and_xor_fusion.place, ...), custom_call_target="tpu_custom_call" | custom-call | flops 24696061952 | bytes 20971520 | tf_op jit(solution)/shard_map/middle/pallas_call | solution.py:354
  131.7 0.0 copy-start.12
  131.7 0.0 all-reduce.3.cloned.1.call-update
  131.7 0.6 copy-done.12
  132.4 106.6 %conditional.1 = (f32[2048,512]{1,0:T(8,128)}, f32[512,256]{1,0:T(8,128)}, f32[512,256]{1,0:T(8,128)}, f32[512,256]{1,0:T(8,128)}) conditional(s32[]{:T(128)} %bitcast.3, f32[2048,512]{1,0:T(8,128)} %get-tuple-element.188, (s32[6]{0:T(128)S(1)}, bf16[8,1024,1024]{2,1,0:T(8,128)(2,1)}, f32[256,2048]{1,0:T(8,128)}, f32[8,1,1024]{2,1,0:T(1,128)S(1)}, ...), branch_computations={%region_3.0_spmd, %region_4.0_spmd} | conditional | flops 68719968256 | bytes 28839448 | solution.py:768
  132.4 0.6 fusion
  133.0 28.5 %attention_backward_own.1 = (f32[2048,512]{1,0:T(8,128)}, f32[256,768]{1,0:T(8,128)}, f32[256,768]{1,0:T(8,128)}) custom-call(s32[1]{0:T(128)} %get-tuple-element.216.core, bf16[8,1024,1024]{2,1,0:T(8,128)(2,1)} %get-tuple-element.35.e_in, f32[256,2048]{1,0:T(8,128)} %get-tuple-element.36.do_in, ...), custom_call_target="tpu_custom_call", output_to_operand_aliasing={{0}: (8, {})} | custom-call | flops 34359738368 | bytes 1000 | tf_op jit(solution)/shard_map/cond/branch_1_fun/attention_backward_own/pallas_call | solution.py:519
  161.5 0.1 collective-permute-start
  162.9 1.0 collective-permute-done
  164.0 0.9 copy-done.4
  164.9 1.5 add.18
  166.5 1.8 collective-permute-start.1
  168.3 15.3 %attention_backward_other.2.gs_in = f32[2048,512]{1,0:T(8,128)} custom-call(s32[1]{0:T(128)} %get-tuple-element.216.core, bf16[8,1024,1024]{2,1,0:T(8,128)(2,1)} %get-tuple-element.47.e_in, f32[256,2048]{1,0:T(8,128)} %get-tuple-element.48.do_in, f32[8,1,1024]{2,1,0:T(1,128)} %get-tuple-element.49.dl_in, ...), custom_call_target="tpu_custom_call", output_to_operand_aliasing={{}: (8, {})} | custom-call | flops 17179869184 | bytes 1000 | tf_op jit(solution)/shard_map/cond/branch_1_fun/attention_backward_other/pallas_call | solution.py:519
  183.6 0.0 collective-permute-done.1
  183.7 1.7 collective-permute-start.2
  185.3 15.2 %attention_backward_other.3 = f32[2048,512]{1,0:T(8,128)} custom-call(s32[1]{0:T(128)} %get-tuple-element.216.core, bf16[8,1024,1024]{2,1,0:T(8,128)(2,1)} %get-tuple-element.47.e_in, f32[256,2048]{1,0:T(8,128)} %get-tuple-element.48.do_in, f32[8,1,1024]{2,1,0:T(1,128)S(1)} %copy-done.14, ...), custom_call_target="tpu_custom_call", output_to_operand_aliasing={{}: (8, {})} | custom-call | flops 17179869184 | bytes 1000 | tf_op jit(solution)/shard_map/cond/branch_1_fun/attention_backward_other/pallas_call | solution.py:519
  200.5 0.0 collective-permute-done.2
  200.5 2.7 collective-permute-start.3
  203.2 15.2 %collective-permute-done.3 = f32[128,768]{1,0:T(8,128)S(1)} collective-permute-done((f32[128,768]{1,0:T(8,128)S(1)}, f32[128,768]{1,0:T(8,128)S(1)}, u32[]{:S(2)}, u32[]{:S(2)}) %collective-permute-start.3) | collective-permute-done | bytes 393248 | tf_op jit(solution)/shard_map/cond/branch_1_fun/ppermute | solution.py:697
  218.5 0.0 copy-start
  218.5 1.1 collective-permute-start.4
  219.6 0.0 collective-permute-start.5
  219.6 14.2 %collective-permute-done.4.refs_1_ = f32[128,768]{1,0:T(8,128)S(1)} collective-permute-done((f32[128,768]{1,0:T(8,128)S(1)}, f32[128,768]{1,0:T(8,128)S(1)}, u32[]{:S(2)}, u32[]{:S(2)}) %collective-permute-start.4) | collective-permute-done | bytes 393248 | tf_op jit(solution)/shard_map/cond/branch_1_fun/ppermute | solution.py:697
  233.9 0.0 collective-permute-start.6
  233.9 1.7 collective-permute-done.6.refs_3_
  235.6 0.7 copy-done.9
  236.3 2.6 finish_qkv.1
  239.0 18.6 %all-reduce.3.cloned.1.call-done = (f32[1024,512]{1,0:T(8,128)}, f32[512,1024]{1,0:T(8,128)}, f32[264,512]{1,0:T(8,128)}) async-done(((f32[1024,512]{1,0:T(8,128)}, f32[512,1024]{1,0:T(8,128)}, f32[264,512]{1,0:T(8,128)}), (f32[1024,512]{1,0:T(8,128)}, f32[512,1024]{1,0:T(8,128)}, f32[264,512]{1,0:T(8,128)})) %all-reduce.3.cloned.1.call-update) | async-done | bytes 4734992 | tf_op jit(solution)/shard_map/psum | solution.py:735
  257.6 5.1 %finish_ff.1 = (f32[1024,512]{1,0:T(8,128)}, f32[512,1024]{1,0:T(8,128)}, f32[256,512]{1,0:T(8,128)}, f32[512]{0:T(512)}, f32[512]{0:T(512)}, /*index=5*/f32[512]{0:T(512)}, f32[512]{0:T(512)}, f32[512]{0:T(512)}) custom-call(f32[1024,512]{1,0:T(8,128)} %get-tuple-element.201.gu_in, f32[512,1024]{1,0:T(8,128)} %get-tuple-element.202.gi_in, ...), custom_call_target="tpu_custom_call" | custom-call | tf_op jit(solution)/shard_map/finish_ff/pallas_call | solution.py:659
  (28 shorter events, 0.2 us)
Async XLA Ops:
  7.2 250.4 %all-reduce.3.cloned.1.call-start = ((), (), s32[]{:S(2)}) async-start(), calls=%async_computation | async-start | bytes 9469952 | tf_op jit(solution)/shard_map/psum | solution.py:735
  10.8 6.3 %copy-start.1 = (bf16[512,256]{1,0:T(8,128)(2,1)S(1)}, bf16[512,256]{1,0:T(8,128)(2,1)}, u32[]{:S(2)}) copy-start(bf16[512,256]{1,0:T(8,128)(2,1)} %wq.3) | copy-start | bytes 786436
  10.8 6.3 %copy-start.2 = (bf16[512,256]{1,0:T(8,128)(2,1)S(1)}, bf16[512,256]{1,0:T(8,128)(2,1)}, u32[]{:S(2)}) copy-start(bf16[512,256]{1,0:T(8,128)(2,1)} %wk.3) | copy-start | bytes 786436
  10.8 6.3 %copy-start.3 = (bf16[512,256]{1,0:T(8,128)(2,1)S(1)}, bf16[512,256]{1,0:T(8,128)(2,1)}, u32[]{:S(2)}) copy-start(bf16[512,256]{1,0:T(8,128)(2,1)} %wv.3) | copy-start | bytes 786436
  10.8 15.2 %collective-permute-start.7 = (f32[128,768]{1,0:T(8,128)}, f32[128,768]{1,0:T(8,128)S(1)}, u32[]{:S(2)}, u32[]{:S(2)}) collective-permute-start(f32[128,768]{1,0:T(8,128)} %get-tuple-element.144), channel_id=1, source_target_pairs={{0,1},{1,0},{2,3},{3,2},{4,5},{5,4},{6,7},{7,6},{8,9},{9,8},{10,11... | collective-permute-start | bytes 1179656 | tf_op jit(solution)/shard_map/ppermute | solution.py:694
  17.0 20.3 %collective-permute-start.9 = (f32[320,512]{1,0:T(8,128)}, f32[320,512]{1,0:T(8,128)}, u32[]{:S(2)}, u32[]{:S(2)}) collective-permute-start(f32[320,512]{1,0:T(8,128)} %get-tuple-element.152), channel_id=1, source_target_pairs={{0,1},{1,0},{2,3},{3,2},{4,5},{5,4},{6,7},{7,6},{8,9},{9,8},{10,11... | collective-permute-start | bytes 1966088 | tf_op jit(solution)/shard_map/ppermute | solution.py:694
  26.0 11.0 %copy-start.5 = (f32[128,768]{1,0:T(8,128)}, f32[128,768]{1,0:T(8,128)S(1)}, u32[]{:S(2)}) copy-start(f32[128,768]{1,0:T(8,128)S(1)} %collective-permute-done.7.refs_0_) | copy-start | bytes 1179652
  26.0 15.2 %collective-permute-start.13 = (f32[128,768]{1,0:T(8,128)S(1)}, f32[128,768]{1,0:T(8,128)S(1)}, u32[]{:S(2)}, u32[]{:S(2)}) collective-permute-start(f32[128,768]{1,0:T(8,128)S(1)} %collective-permute-done.7.refs_0_), channel_id=1, source_target_pairs={{0,2},{2,0},{4,6},{6,4},{8,10},{10,8},{12,14},{14,12},{16,18},{18,... | collective-permute-start | bytes 1179656 | tf_op jit(solution)/shard_map/ppermute | solution.py:697
  26.1 11.9 %collective-permute-start.8 = (f32[128,768]{1,0:T(8,128)S(1)}, f32[128,768]{1,0:T(8,128)}, u32[]{:S(2)}, u32[]{:S(2)}) collective-permute-start(f32[128,768]{1,0:T(8,128)S(1)} %collective-permute-done.7.refs_0_), channel_id=1, source_target_pairs={{0,4},{2,6},{4,0},{6,2},{8,12},{10,14},{12,8},{14,10},{16,20},{18,... | collective-permute-start | bytes 1179656 | tf_op jit(solution)/shard_map/ppermute | solution.py:697
  38.0 3.3 %collective-permute-start.14 = (f32[128,768]{1,0:T(8,128)}, f32[128,768]{1,0:T(8,128)}, u32[]{:S(2)}, u32[]{:S(2)}) collective-permute-start(f32[128,768]{1,0:T(8,128)} %collective-permute-done.8.refs_1_), channel_id=1, source_target_pairs={{0,2},{2,0},{4,6},{6,4},{8,10},{10,8},{12,14},{14,12},{16,18},{18,... | collective-permute-start | bytes 1179656 | tf_op jit(solution)/shard_map/ppermute | solution.py:697
  38.0 17.5 %collective-permute-start.11 = (f32[320,512]{1,0:T(8,128)}, f32[320,512]{1,0:T(8,128)}, u32[]{:S(2)}, u32[]{:S(2)}) collective-permute-start(f32[320,512]{1,0:T(8,128)} %collective-permute-done.9.i0), channel_id=1, source_target_pairs={{0,4},{2,6},{4,0},{6,2},{8,12},{10,14},{12,8},{14,10},{16,20},{18,... | collective-permute-start | bytes 1966088 | tf_op jit(solution)/shard_map/ppermute | solution.py:697
  39.7 14.4 %collective-permute-start.12 = (f32[256,512]{1,0:T(8,128)}, f32[256,512]{1,0:T(8,128)}, u32[]{:S(2)}, u32[]{:S(2)}) collective-permute-start(f32[256,512]{1,0:T(8,128)} %get-tuple-element.161), channel_id=1, source_target_pairs={{0,1},{1,0},{2,3},{3,2},{4,5},{5,4},{6,7},{7,6},{8,9},{9,8},{10,11... | collective-permute-start | bytes 1572872 | tf_op jit(solution)/shard_map/ppermute | solution.py:694
  41.2 25.4 %collective-permute-start.10 = (f32[320,512]{1,0:T(8,128)}, f32[320,512]{1,0:T(8,128)}, u32[]{:S(2)}, u32[]{:S(2)}) collective-permute-start(f32[320,512]{1,0:T(8,128)} %collective-permute-done.9.i0), channel_id=1, source_target_pairs={{0,2},{2,0},{4,6},{6,4},{8,10},{10,8},{12,14},{14,12},{16,18},{18,... | collective-permute-start | bytes 1966088 | tf_op jit(solution)/shard_map/ppermute | solution.py:697
  41.2 0.7 copy-start.6
  43.4 14.3 %copy-start.10 = (bf16[512,256]{1,0:T(8,128)(2,1)}, bf16[512,256]{1,0:T(8,128)(2,1)S(1)}, u32[]{:S(2)}) copy-start(bf16[512,256]{1,0:T(8,128)(2,1)S(1)} %get-tuple-element.164.wk) | copy-start | bytes 786436
  43.4 14.3 %copy-start.11 = (bf16[512,256]{1,0:T(8,128)(2,1)}, bf16[512,256]{1,0:T(8,128)(2,1)S(1)}, u32[]{:S(2)}) copy-start(bf16[512,256]{1,0:T(8,128)(2,1)S(1)} %get-tuple-element.165.wv) | copy-start | bytes 786436
  55.5 14.7 %collective-permute-start.15 = (f32[320,512]{1,0:T(8,128)}, f32[320,512]{1,0:T(8,128)}, u32[]{:S(2)}, u32[]{:S(2)}) collective-permute-start(f32[320,512]{1,0:T(8,128)} %collective-permute-done.11.i1), channel_id=1, source_target_pairs={{0,2},{2,0},{4,6},{6,4},{8,10},{10,8},{12,14},{14,12},{16,18},{18,... | collective-permute-start | bytes 1966088 | tf_op jit(solution)/shard_map/ppermute | solution.py:697
  55.5 11.1 %collective-permute-start.17 = (f32[256,512]{1,0:T(8,128)}, f32[256,512]{1,0:T(8,128)}, u32[]{:S(2)}, u32[]{:S(2)}) collective-permute-start(f32[256,512]{1,0:T(8,128)} %collective-permute-done.12.o0), channel_id=1, source_target_pairs={{0,2},{2,0},{4,6},{6,4},{8,10},{10,8},{12,14},{14,12},{16,18},{18,... | collective-permute-start | bytes 1572872 | tf_op jit(solution)/shard_map/ppermute | solution.py:697
  56.0 14.1 %collective-permute-start.16 = (f32[256,512]{1,0:T(8,128)}, f32[256,512]{1,0:T(8,128)}, u32[]{:S(2)}, u32[]{:S(2)}) collective-permute-start(f32[256,512]{1,0:T(8,128)} %collective-permute-done.12.o0), channel_id=1, source_target_pairs={{0,4},{2,6},{4,0},{6,2},{8,12},{10,14},{12,8},{14,10},{16,20},{18,... | collective-permute-start | bytes 1572872 | tf_op jit(solution)/shard_map/ppermute | solution.py:697
  70.1 2.1 collective-permute-start.18
  72.2 0.8 copy-start.13
  131.7 0.7 copy-start.12
  161.5 2.5 collective-permute-start
  164.0 0.9 copy-start.4
  166.5 17.1 %collective-permute-start.1 = (f32[128,768]{1,0:T(8,128)S(1)}, f32[128,768]{1,0:T(8,128)S(1)}, u32[]{:S(2)}, u32[]{:S(2)}) collective-permute-start(f32[128,768]{1,0:T(8,128)S(1)} %constant_dynamic-slice_fusion), channel_id=1, source_target_pairs={{0,4},{2,6},{4,0},{6,2},{8,12},{10,14},{12,8},{14,10},{16,20},{18,... | collective-permute-start | bytes 1179656 | tf_op jit(solution)/shard_map/cond/branch_1_fun/ppermute | solution.py:697
  168.3 17.0 %copy-start.14 = (f32[8,1,1024]{2,1,0:T(1,128)S(1)}, f32[8,1,1024]{2,1,0:T(1,128)}, u32[]{:S(2)}) copy-start(f32[8,1,1024]{2,1,0:T(1,128)} %get-tuple-element.49.dl_in) | copy-start | bytes 98308 | tf_op jit(solution)/shard_map/cond
  183.7 16.8 %collective-permute-start.2 = (f32[128,768]{1,0:T(8,128)S(1)}, f32[128,768]{1,0:T(8,128)S(1)}, u32[]{:S(2)}, u32[]{:S(2)}) collective-permute-start(f32[128,768]{1,0:T(8,128)S(1)} %dynamic-slice_add_fusion), channel_id=1, source_target_pairs={{0,8},{2,18},{4,12},{6,22},{8,0},{10,26},{12,4},{14,30},{16,24},{1... | collective-permute-start | bytes 1179656 | tf_op jit(solution)/shard_map/cond/branch_1_fun/ppermute | solution.py:697
  200.5 17.9 %collective-permute-start.3 = (f32[128,768]{1,0:T(8,128)S(1)}, f32[128,768]{1,0:T(8,128)S(1)}, u32[]{:S(2)}, u32[]{:S(2)}) collective-permute-start(f32[128,768]{1,0:T(8,128)S(1)} %add.22), channel_id=1, source_target_pairs={{0,16},{2,10},{4,20},{6,14},{8,24},{10,2},{12,28},{14,6},{16,0},{1... | collective-permute-start | bytes 1179656 | tf_op jit(solution)/shard_map/cond/branch_1_fun/ppermute | solution.py:697
  218.5 17.1 %copy-start = (f32[128,768]{1,0:T(8,128)}, f32[128,768]{1,0:T(8,128)S(1)}, u32[]{:S(2)}) copy-start(f32[128,768]{1,0:T(8,128)S(1)} %add.23.refs_0_) | copy-start | bytes 1179652 | tf_op jit(solution)/shard_map/cond
  218.5 15.4 %collective-permute-start.4 = (f32[128,768]{1,0:T(8,128)S(1)}, f32[128,768]{1,0:T(8,128)S(1)}, u32[]{:S(2)}, u32[]{:S(2)}) collective-permute-start(f32[128,768]{1,0:T(8,128)S(1)} %add.23.refs_0_), channel_id=1, source_target_pairs={{0,4},{2,6},{4,0},{6,2},{8,12},{10,14},{12,8},{14,10},{16,20},{18,... | collective-permute-start | bytes 1179656 | tf_op jit(solution)/shard_map/cond/branch_1_fun/ppermute | solution.py:697
  219.6 14.3 %collective-permute-start.5 = (f32[128,768]{1,0:T(8,128)S(1)}, f32[128,768]{1,0:T(8,128)S(1)}, u32[]{:S(2)}, u32[]{:S(2)}) collective-permute-start(f32[128,768]{1,0:T(8,128)S(1)} %add.23.refs_0_), channel_id=1, source_target_pairs={{0,2},{2,0},{4,6},{6,4},{8,10},{10,8},{12,14},{14,12},{16,18},{18,... | collective-permute-start | bytes 1179656 | tf_op jit(solution)/shard_map/cond/branch_1_fun/ppermute | solution.py:697
  233.9 1.7 copy-start.7
  233.9 1.7 collective-permute-start.6
  233.9 1.7 copy-start.8
  235.6 0.8 copy-start.9
Sparse Core Ops, SparseCore 0:
  131.8 125.7 all-reduce.2
